TPU v7x, 128 devices: a whole 4x4x4 slice. The times are simulated.
128 devices in a mesh: dp: 4 (over y_lo, core), mp: 32 (over z, y_hi, x).
Axes of the slice: x: 4, y: 4 (y_hi: 2, y_lo: 2; y = y_hi * 2 + y_lo), z: 4, core: 2. Of those that a mesh axis runs over, the one named last changes fastest.
Arguments:
- hidden_states: bfloat16 [4096, 16384], P('dp', 'mp'), may hold values from -400 to 400, as said below
- norm_gain: bfloat16 [16384], P('mp'), may hold values from 0.5 to 1.5
- damping: float32 [16384], P('mp'), may hold values from 0.05 to 0.5
Outputs:
- hessian: float32 [2048, 16384], P('dp', 'mp')
- factor_rows: float32 [1024, 16384], P('dp', 'mp')
- updated_rows: float32 [1024, 16384], P('dp', 'mp')
Inputs may be any that keep to these rules, and one draw needn't show every extreme that they name: `hidden_states`: activations with token scales and feature scales of different sizes.
All inputs are finite; a program needn't handle non-finite values.
Results may differ from a plain program's by a relative error of at most 0.0038.
Values may be sent and summed in bfloat16 or wider, within the bound.
A program may use at most 128 MiB of HBM per device.

v0:
```python
import jax
import jax.numpy as jnp
from jax import lax
from jax.sharding import PartitionSpec as P

D = 16384
PANEL = 1024


def spread(value, axis, source):
    kept = jnp.where(lax.axis_index(axis) == source, value, 0).astype(value.dtype)
    return lax.psum(kept, axis)


def place_cols(source, first_col, span_cols):
    source_cols = source.shape[1]
    padded = jnp.pad(source, ((0, 0), (span_cols, span_cols)))
    offset_cols = jnp.clip(first_col, -source_cols, span_cols)
    return lax.dynamic_slice_in_dim(padded, span_cols - offset_cols, span_cols, 1)


def add_damping(own_block, damping, first_col):
    row_ids = jnp.arange(own_block.shape[0], dtype=jnp.int32)
    col_ids = first_col + jnp.arange(own_block.shape[1], dtype=jnp.int32)
    on_diagonal = row_ids[:, None] == col_ids[None, :]
    return own_block + jnp.where(on_diagonal, damping[None, :], jnp.float32(0.0))


def body(hidden_states, norm_gain, damping):
    tok_rows, feature_cols = hidden_states.shape
    group_index = lax.axis_index("dp")
    column_index = lax.axis_index("mp")
    group_count = lax.axis_size("dp")
    span_rows = 2 * PANEL
    values = hidden_states.astype(jnp.float32)
    ssq = lax.psum(jnp.sum(values * values, axis=1), "mp")
    inverse_rms = lax.rsqrt(ssq / D + 1e-05)
    normed = (values * inverse_rms[:, None] * norm_gain.astype(jnp.float32)[None, :]).astype(
        jnp.bfloat16
    )
    root_count = max(1, span_rows // feature_cols)
    pieces = [spread(normed, "mp", root) for root in range(root_count)]
    window = jnp.concatenate(pieces, axis=1)
    tokens_all = tok_rows * group_count
    block_rows = span_rows // group_count
    first_row = group_index * block_rows
    first_col = column_index * feature_cols
    product = lax.dot_general(
        window, normed, (((0,), (0,)), ((), ())), preferred_element_type=jnp.float32
    )
    column_slab = lax.psum(product / tokens_all, "dp")
    column_slab = add_damping(column_slab, damping, first_col)
    own_block = lax.dynamic_slice_in_dim(column_slab, first_row, block_rows, 0)
    placed_piece = place_cols(own_block, first_col, PANEL)
    canvas = jnp.zeros((PANEL + block_rows, PANEL), jnp.float32)
    canvas = lax.dynamic_update_slice(canvas, placed_piece, (jnp.minimum(first_row, PANEL), 0))
    diagonal_block = lax.psum(canvas[:PANEL], ("dp", "mp"))
    lower_factor = jnp.linalg.cholesky(diagonal_block)
    upper_rows = lax.linalg.triangular_solve(
        lower_factor, column_slab[:PANEL], left_side=True, lower=True
    )
    quarter_rows = PANEL // group_count
    factor_rows = lax.dynamic_slice_in_dim(upper_rows, group_index * quarter_rows, quarter_rows, 0)
    next_block = lax.psum(place_cols(upper_rows, first_col - PANEL, PANEL), "mp")
    next_part = lax.dynamic_slice_in_dim(next_block, group_index * quarter_rows, quarter_rows, 1)
    second_rows = lax.dynamic_slice_in_dim(
        column_slab, PANEL + group_index * quarter_rows, quarter_rows, 0
    )
    updated_rows = second_rows - jnp.dot(next_part.T, upper_rows, precision=lax.Precision.HIGHEST)
    return (own_block, factor_rows, updated_rows)


def solution(mesh):
    return jax.shard_map(
        body,
        mesh=mesh,
        in_specs=(P("dp", "mp"), P("mp"), P("mp")),
        out_specs=(P("dp", "mp"), P("dp", "mp"), P("dp", "mp")),
        check_vma=False,
    )
```

profile of v0, /device:TPU:1, one launch (start us, length us, event | category | flops | bytes accessed | tf_op | source)
XLA Modules:
  0.0 1456.8 jit_solution(2659031497410246349)
XLA Ops:
  8.7 84.4 %psum.56 = f32[1024]{0:T(1024)S(1)} all-reduce(f32[1024]{0:T(1024)S(1)} %fusion.12), channel_id=1, replica_groups=mesh['dp'=4,'mp'=32] {'mp'}, use_global_device_ids=true, to_apply=%region_1.0 | all-reduce | flops 1024 | bytes 8192 | tf_op jit(solution)/shard_map/psum | solution.py:36
  97.7 353.9 %all-reduce.15.cloned.1.call-done = (bf16[1024,512]{1,0:T(8,128)(2,1)}, bf16[1024,512]{1,0:T(8,128)(2,1)}, bf16[1024,512]{1,0:T(8,128)(2,1)}, bf16[1024,512]{1,0:T(8,128)(2,1)}) async-done(((bf16[1024,512]{1,0:T(8,128)(2,1)}, bf16[1024,512]{1,0:T(8,128)(2,1)}, bf16[1024,512]{1,0:T(8,128)(2,1)}, bf16[1024,512]{1,0:T(8,128)(2,1)}), (bf16[1024,512]{1,0:T(8,128)(2,1)}, bf16[1024,512]{1,0:T(8,128)(2,1)}, ...) | async-done | bytes 4194320 | tf_op jit(solution)/shard_map/psum | solution.py:12
  451.6 6.6 fusion.9
  458.2 112.4 %all-reduce.9.cloned.1.call-done = f32[2048,512]{0,1:T(8,128)} async-done(((f32[2048,512]{0,1:T(8,128)}), f32[2048,512]{0,1:T(8,128)}) %all-reduce.9.cloned.1.call-update) | async-done | bytes 4194320 | tf_op jit(solution)/shard_map/psum | solution.py:51
  579.5 10.5 dynamic_update_slice.3
  594.9 154.8 %all-reduce.11.cloned.1.call-done = f32[1024,1024]{0,1:T(8,128)} async-done(((f32[1024,1024]{0,1:T(8,128)}), f32[1024,1024]{0,1:T(8,128)}) %all-reduce.11.cloned.1.call-update) | async-done | bytes 4194320 | tf_op jit(solution)/shard_map/psum | solution.py:57
  761.9 11.7 cholesky.223
  776.2 9.8 custom-call.62
  789.9 11.9 cholesky.244
  802.4 9.8 custom-call.63
  815.6 11.7 cholesky.468
  828.6 9.8 custom-call.64
  841.9 11.9 cholesky.487
  855.1 9.8 custom-call.65
  868.4 11.7 cholesky.506
  881.5 10.2 custom-call.66
  895.0 11.7 cholesky.526
  907.9 9.8 custom-call.67
  920.8 11.9 cholesky.546
  934.0 9.8 custom-call.68
  946.4 11.7 cholesky.564
  969.9 23.2 %while.1 = (s32[]{:T(128)}, f32[1024,1024]{1,0:T(8,128)}, s32[8,2]{0,1:T(2,128)S(1)}, f32[8,128,128]{2,1,0:T(8,128)S(1)}, s32[]{:T(128)}) while((s32[]{:T(128)}, f32[1024,1024]{1,0:T(8,128)}, s32[8,2]{0,1:T(2,128)S(1)}, f32[8,128,128]{2,1,0:T(8,128)S(1)}, s32[]{:T(128)}) %tuple.65), condition=%wide.while_cond, body=%wide.while_body.sunk | while | flops 2 | bytes 131181 | solution.py:59
  993.1 79.4 %custom-call.69 = f32[8,128,128]{1,2,0:T(8,128)} custom-call(f32[8,128,128]{2,1,0:T(8,128)S(1)} %get-tuple-element.10), custom_call_target="InvertDiagBlocksLowerTriangular" | custom-call | tf_op jit(solution)/shard_map/triangular_solve | solution.py:59
  1103.9 340.1 %all-reduce.13.cloned.1.call-done = f32[1024,1024]{1,0:T(8,128)} async-done(((f32[1024,1024]{1,0:T(8,128)}), f32[1024,1024]{1,0:T(8,128)}) %all-reduce.13.cloned.1.call-update) | async-done | bytes 4194320 | tf_op jit(solution)/shard_map/psum | solution.py:64
  (115 shorter events, 131.8 us)
Async XLA Ops:
  7.2 444.4 %all-reduce.15.cloned.1.call-start = ((), (), s32[]{:S(2)}) async-start(), calls=%async_computation.3 | async-start | bytes 8388608 | tf_op jit(solution)/shard_map/psum | solution.py:12
  93.9 357.7 %copy-start.2 = (bf16[1024,512]{1,0:T(8,128)(2,1)S(1)}, bf16[1024,512]{1,0:T(8,128)(2,1)}, u32[]{:S(2)}) copy-start(bf16[1024,512]{1,0:T(8,128)(2,1)} %param.3) | copy-start | bytes 3145732
  97.7 473.0 %all-reduce.9.cloned.1.call-start = ((), (), s32[]{:S(2)}) async-start(), calls=%async_computation | async-start | bytes 8388608 | tf_op jit(solution)/shard_map/psum | solution.py:51
  458.1 112.5 %copy-start.4 = (f32[512]{0:T(512)S(1)}, f32[512]{0:T(512)}, u32[]{:S(2)}) copy-start(f32[512]{0:T(512)} %param.5) | copy-start | bytes 6148
  458.1 291.5 %all-reduce.11.cloned.1.call-start = ((), (), s32[]{:S(2)}) async-start(), calls=%async_computation.1 | async-start | bytes 8388608 | tf_op jit(solution)/shard_map/psum | solution.py:57
  573.4 2.0 copy-start
  594.9 849.2 %all-reduce.13.cloned.1.call-start = ((), (), s32[]{:S(2)}) async-start(), calls=%async_computation.2 | async-start | bytes 8388608 | tf_op jit(solution)/shard_map/psum | solution.py:64
  759.9 1.9 copy-start.1
  1072.5 6.5 copy-start.3
Sparse Core Ops, SparseCore 0:
  97.8 353.7 all-reduce.14
  458.3 112.3 all-reduce.8
  595.0 154.6 all-reduce.10
  1101.9 342.0 all-reduce.12
where the time goes:
time: 1480 us; the launch traced here: 1460 us
  waiting for transfers between devices  961 us (65%)
  other arithmetic  270 us (18%)
  blocking collectives  84.4 us (6%)
  local copies, waits for them, and re-layouts  61.2 us (4%)
  matrix products  60.4 us (4%)
  between operations  19.7 us (1%)
    psum x1, waiting for transfers between devices, spread(): return lax.psum(kept, axis)  354 us
    psum x1, waiting for transfers between devices, body(): lax.psum(place_cols(upper_rows, first_col - PANEL, PANEL), 'mp')  340 us
    another operation x30, other arithmetic, body(): lower_factor = jnp.linalg.cholesky(diagonal_block)  172 us
    psum x1, waiting for transfers between devices, body(): diagonal_block = lax.psum(canvas[:PANEL], ('dp', 'mp'))  155 us
    psum x1, waiting for transfers between devices, body(): column_slab = lax.psum(product / tokens_all, 'dp')  112 us
    psum x1, blocking collectives, body(): ssq = lax.psum(jnp.sum(values * values, axis=1), 'mp')  84.4 us
    another operation x3, other arithmetic, body(): lax.linalg.triangular_solve(lower_factor, column_slab[:PANEL], left_side=...  84.2 us
  transfers between devices with their start and end apart: 4, of which 4 were waited for; matrix products, arithmetic and copies ran while one was open for 0% of the time, Pallas kernels for 0%

commit v1 on v0

v1 whole, which is shorter than its diff:
```python
import functools

import jax
import jax.numpy as jnp
from jax import lax
from jax.experimental import pallas as pl
from jax.experimental.pallas import tpu as pltpu
from jax.sharding import PartitionSpec as P

D = 16384
PANEL = 1024
TOKENS = 4096
MESH = pl.DeviceIdType.MESH
HI = lax.Precision.HIGHEST
F32 = jnp.float32
VM = pl.BlockSpec(memory_space=pltpu.VMEM)


def params(**kw):
    return pltpu.CompilerParams(vmem_limit_bytes=56 * 2**20, **kw)


def spot():
    mp = lax.axis_index("mp")
    return lax.axis_index("dp"), mp // 8, (mp // 4) % 2, mp % 4


def at(dp, z, h, x):
    return (dp, z * 8 + h * 4 + x)


def greet(partners):
    barrier = pltpu.get_barrier_semaphore()
    for p in partners:
        pl.semaphore_signal(barrier, inc=1, device_id=p, device_id_type=MESH)
    pl.semaphore_wait(barrier, len(partners))


def spread_kernel(x_ref, aux_ref, w_ref, auxs_ref, ssq_ref, sx, sz, sh, s0s, s0r, ps, pr, qs, qr):
    dp, z, h, x = spot()
    column = [at(dp, (z + q // 2) % 4, (h + q % 2) % 2, x) for q in range(1, 8)]
    ring_x = [at(dp, z, h, (x + j) % 4) for j in range(1, 4)]
    ring_z = [at(dp, (z + j) % 4, h, x) for j in range(1, 4)]
    peer_h = at(dp, z, 1 - h, x)
    greet(column + ring_x)

    def copy(src, dst, ss, rs, dev):
        return pltpu.make_async_remote_copy(src_ref=src, dst_ref=dst, send_sem=ss, recv_sem=rs,
                                            device_id=dev, device_id_type=MESH)

    def rows_of(zz, hh):
        return pl.multiple_of(zz * 128 + hh * 64, 64)

    is_source = (z == 0) & (h == 0)

    def scatter(q):
        a = (q // 2) * 128 + (q % 2) * 64
        return [
            copy(aux_ref, auxs_ref.at[x], s0s.at[3 * q + 2], s0r.at[2], column[q - 1]),
            copy(x_ref.at[pl.ds(a, 64)], w_ref.at[x, pl.ds(a, 64)], s0s.at[3 * q], s0r.at[0], column[q - 1]),
            copy(x_ref.at[pl.ds(512 + a, 64)], w_ref.at[x, pl.ds(512 + a, 64)], s0s.at[3 * q + 1], s0r.at[1],
                 column[q - 1]),
        ]

    @pl.when(is_source)
    def _():
        for q in range(1, 8):
            for c in scatter(q):
                c.start()
        w_ref[x, 0:64] = x_ref[0:64]
        w_ref[x, 512:576] = x_ref[512:576]
        auxs_ref[x] = aux_ref[...]

    part = jnp.zeros((1024, 128), F32)
    for i in range(4):
        v = x_ref[:, 128 * i:128 * i + 128].astype(F32)
        part = part + v * v
    line = jnp.sum(part.T, axis=0, keepdims=True)
    for i in range(8):
        sx[x, i:i + 1, :] = line[:, 128 * i:128 * i + 128]
    sum_x = [copy(sx.at[x], sx.at[x], qs.at[j], qr.at[j], ring_x[j]) for j in range(3)]
    for c in sum_x:
        c.start()

    @pl.when(jnp.logical_not(is_source))
    def _():
        for c in scatter(1):
            c.wait_recv()

    own = rows_of(z, h)
    pair = pl.multiple_of(z * 128, 128)
    half_a = w_ref.at[x, pl.ds(own, 64)]
    half_b = w_ref.at[x, pl.ds(512 + own, 64)]
    step_h = [copy(half_a, half_a, ps.at[0], pr.at[0], peer_h), copy(half_b, half_b, ps.at[1], pr.at[1], peer_h)]
    for c in step_h:
        c.start()
    step_aux = [copy(auxs_ref.at[x], auxs_ref.at[x], ps.at[2 + j], pr.at[2 + j], ring_x[j]) for j in range(3)]
    for c in step_aux:
        c.start()
    for c in sum_x:
        c.wait_recv()
    sz[z] = (sx[0] + sx[1]) + (sx[2] + sx[3])
    sum_z = [copy(sz.at[z], sz.at[z], qs.at[3 + j], qr.at[3 + j], ring_z[j]) for j in range(3)]
    for c in sum_z:
        c.start()

    both_a = w_ref.at[x, pl.ds(pair, 128)]
    both_b = w_ref.at[x, pl.ds(512 + pair, 128)]
    step_2a = [copy(both_a, both_a, ps.at[5 + j], pr.at[5 + j], ring_x[j]) for j in range(3)]
    step_2b = [copy(both_b, both_b, ps.at[8 + j], pr.at[8 + j], ring_z[j]) for j in range(3)]
    step_h[0].wait_recv()
    for c in step_2a:
        c.start()
    step_h[1].wait_recv()
    for c in step_2b:
        c.start()

    for c in sum_z:
        c.wait_recv()
    sh[h] = (sz[0] + sz[1]) + (sz[2] + sz[3])
    sum_h = copy(sh.at[h], sh.at[h], qs.at[6], qr.at[6], peer_h)
    sum_h.start()

    all_a = w_ref.at[:, pl.ds(pair, 128)]
    all_b = w_ref.at[x, pl.ds(512, 512)]
    step_3a = [copy(all_a, all_a, ps.at[11 + j], pr.at[11 + j], ring_z[j]) for j in range(3)]
    step_3b = [copy(all_b, all_b, ps.at[14 + j], pr.at[14 + j], ring_x[j]) for j in range(3)]
    for c in step_2a:
        c.wait_recv()
    for c in step_3a:
        c.start()
    for c in step_2b:
        c.wait_recv()
    for c in step_3b:
        c.start()
    sum_h.wait_recv()
    ssq_ref[...] = sh[0] + sh[1]
    for c in step_aux + step_3a + step_3b:
        c.wait_recv()
    for c in sum_x + sum_z + [sum_h] + step_h + step_aux + step_2a + step_2b + step_3a + step_3b:
        c.wait_send()

    @pl.when(is_source)
    def _():
        for q in range(1, 8):
            for c in scatter(q):
                c.wait_send()


def spread(hidden, aux):
    return pl.pallas_call(
        spread_kernel,
        out_shape=(
            jax.ShapeDtypeStruct((4, 1024, 512), jnp.bfloat16),
            jax.ShapeDtypeStruct((4, 8, 512), F32),
            jax.ShapeDtypeStruct((8, 128), F32),
        ),
        in_specs=[VM, VM],
        out_specs=(VM, VM, VM),
        scratch_shapes=[
            pltpu.VMEM((4, 8, 128), F32),
            pltpu.VMEM((4, 8, 128), F32),
            pltpu.VMEM((2, 8, 128), F32),
            pltpu.SemaphoreType.DMA((24,)),
            pltpu.SemaphoreType.DMA((3,)),
            pltpu.SemaphoreType.DMA((17,)),
            pltpu.SemaphoreType.DMA((17,)),
            pltpu.SemaphoreType.DMA((7,)),
            pltpu.SemaphoreType.DMA((7,)),
        ],
        compiler_params=params(collective_id=0, has_side_effects=True),
        name="spread_window",
    )(hidden, aux)


def dot_t(a, b, precision=None):
    return lax.dot_general(a, b, (((0,), (0,)), ((), ())), precision=precision, preferred_element_type=F32)


def dot(a, b):
    return jnp.dot(a, b, precision=HI, preferred_element_type=F32)


def gram_kernel(w_ref, auxs_ref, ssq_ref, x_ref, aux_ref, slab_ref, share_ref, wn, xn, rms, wide):
    _, z, _, x = spot()
    inverse = lax.rsqrt(ssq_ref[...] / D + 1e-05)
    for i in range(8):
        rms[128 * i:128 * i + 128, :] = jnp.broadcast_to(inverse[i:i + 1, :], (128, 128)).T

    @pl.loop(0, 8)
    def _(i):
        rows = pl.ds(pl.multiple_of(i * 128, 128), 128)
        scale = jnp.concatenate([rms[rows, :]] * 4, axis=1)
        xn[rows, :] = (x_ref[rows, :].astype(F32) * scale * aux_ref[0:1, :]).astype(jnp.bfloat16)
        for b in range(4):
            wn[b, rows, :] = (w_ref[b, rows, :].astype(F32) * scale * auxs_ref[b, 0:1, :]).astype(jnp.bfloat16)

    s = z * 4 + x
    strip = wn[s // 8, :, pl.ds(pl.multiple_of(((s % 8) // 2) * 128, 128), 128)]
    for b in range(4):
        wide[:, 512 * b:512 * b + 512] = dot_t(strip, wn[b]) * (1.0 / TOKENS)
    share_ref[...] = wide[pl.ds(pl.multiple_of((s % 2) * 64, 64), 64), :]

    @pl.loop(0, 16)
    def _(i):
        left = wn[i // 4, :, pl.ds(pl.multiple_of((i % 4) * 128, 128), 128)]
        slab_ref[pl.ds(pl.multiple_of(i * 128, 128), 128), :] = dot_t(left, xn[...]) * (1.0 / TOKENS)


def gram(w, auxs, ssq, hidden, aux):
    return pl.pallas_call(
        gram_kernel,
        out_shape=(jax.ShapeDtypeStruct((2048, 512), F32), jax.ShapeDtypeStruct((64, 2048), F32)),
        in_specs=[VM] * 5,
        out_specs=(VM, VM),
        scratch_shapes=[
            pltpu.VMEM((4, 1024, 512), jnp.bfloat16),
            pltpu.VMEM((1024, 512), jnp.bfloat16),
            pltpu.VMEM((1024, 128), F32),
            pltpu.VMEM((128, 2048), F32),
        ],
        compiler_params=params(),
        name="partial_gram",
    )(w, auxs, ssq, hidden, aux)


def join_kernel(slab_ref, share_ref, g_ref, p_ref, other, share_in, share_sum, share_y, ss, rs):
    dp, z, h, x = spot()
    c, y = dp % 2, dp // 2
    peer_c = at(y * 2 + 1 - c, z, h, x)
    peer_y = at((1 - y) * 2 + c, z, h, x)
    ring_x = [at(dp, z, h, (x + j) % 4) for j in range(1, 4)]
    ring_z = [at(dp, (z + j) % 4, h, x) for j in range(1, 4)]
    greet([peer_c, peer_y] + ring_x + ring_z)

    def copy(src, dst, i, dev):
        return pltpu.make_async_remote_copy(src_ref=src, dst_ref=dst, send_sem=ss.at[i], recv_sem=rs.at[i],
                                            device_id=dev, device_id_type=MESH)

    to_core = copy(share_ref.at[pl.ds(pl.multiple_of(32 * (1 - c), 32), 32)], share_in, 0, peer_c)
    to_core.start()
    spans = [(512 * (1 - c), 0, 512), (1024 + 256 * (1 - c), 512, 256), (1536 + 256 * (1 - c), 768, 256)]
    slabs = [
        copy(slab_ref.at[pl.ds(pl.multiple_of(a, 256), n)], other.at[pl.ds(b, n)], 1 + i, peer_c)
        for i, (a, b, n) in enumerate(spans)
    ]
    to_core.wait_recv()
    share_sum[...] = share_ref[pl.ds(pl.multiple_of(32 * c, 32), 32), :] + share_in[...]
    give = pl.ds(pl.multiple_of(1024 + 512 * (1 - y), 512), 512)
    keep = pl.ds(pl.multiple_of(1024 + 512 * y, 512), 512)
    to_y = [
        copy(share_sum.at[:, pl.ds(0, 1024)], share_y.at[:, pl.ds(0, 1024)], 4, peer_y),
        copy(share_sum.at[:, give], share_y.at[:, pl.ds(1024, 512)], 5, peer_y),
    ]
    for k in to_y:
        k.start()
    for k in slabs:
        k.start()
    for k in to_y:
        k.wait_recv()
    g_ref[z, x, c, :, 0:1024] = share_sum[:, 0:1024] + share_y[:, 0:1024]
    g_ref[z, x, c, :, 1024:1536] = share_sum[:, keep] + share_y[:, 1024:1536]

    first, second = pl.ds(0, 16), pl.ds(16, 16)
    one_a, one_b = g_ref.at[z, x, c, first], g_ref.at[z, x, c, second]
    step_1a = [copy(one_a, one_a, 6 + j, ring_x[j]) for j in range(3)]
    step_1b = [copy(one_b, one_b, 9 + j, ring_z[j]) for j in range(3)]
    for k in step_1a + step_1b:
        k.start()
    row_a, row_b = g_ref.at[z, :, c, first], g_ref.at[:, x, c, second]
    step_2a = [copy(row_a, row_a, 12 + j, ring_z[j]) for j in range(3)]
    step_2b = [copy(row_b, row_b, 15 + j, ring_x[j]) for j in range(3)]
    for k in step_1a:
        k.wait_recv()
    for k in step_2a:
        k.start()
    for k in step_1b:
        k.wait_recv()
    for k in step_2b:
        k.start()
    for k in slabs:
        k.wait_recv()
    p_ref[0:512, :] = slab_ref[pl.ds(pl.multiple_of(512 * c, 512), 512), :] + other[0:512, :]
    p_ref[512:768, :] = slab_ref[pl.ds(pl.multiple_of(1024 + 256 * c, 256), 256), :] + other[512:768, :]
    p_ref[768:1024, :] = slab_ref[pl.ds(pl.multiple_of(1536 + 256 * c, 256), 256), :] + other[768:1024, :]
    for k in step_2a:
        k.wait_recv()
    full_a, full_b = g_ref.at[:, :, c, first], g_ref.at[:, :, c, second]
    last_a = copy(full_a, full_a, 18, peer_c)
    last_a.start()
    for k in step_2b:
        k.wait_recv()
    last_b = copy(full_b, full_b, 19, peer_c)
    last_b.start()
    last_a.wait_recv()
    last_b.wait_recv()
    for k in [to_core] + slabs + to_y + step_1a + step_1b + step_2a + step_2b + [last_a, last_b]:
        k.wait_send()


def join(slab, share):
    return pl.pallas_call(
        join_kernel,
        out_shape=(jax.ShapeDtypeStruct((4, 4, 2, 32, 1536), F32), jax.ShapeDtypeStruct((1024, 512), F32)),
        in_specs=[VM, VM],
        out_specs=(VM, VM),
        scratch_shapes=[
            pltpu.VMEM((1024, 512), F32),
            pltpu.VMEM((32, 2048), F32),
            pltpu.VMEM((32, 2048), F32),
            pltpu.VMEM((32, 1536), F32),
            pltpu.SemaphoreType.DMA((20,)),
            pltpu.SemaphoreType.DMA((20,)),
        ],
        compiler_params=params(collective_id=1, has_side_effects=True),
        name="join_window",
    )(slab, share)


def lane_of(v, j):
    return jnp.broadcast_to(v[:, j:j + 1], (8, 128))


def row_of(v, r):
    return jnp.broadcast_to(v[r:r + 1, :], (8, 128))


def factor_block(groups, lane, sub):
    done = [None] * 16
    groups = list(groups)
    for p in range(16):
        base = 8 * p
        here = groups[p]
        inside = (lane >= base) & (lane < base + 8)
        cols = [lane_of(here, base + t) for t in range(8)]
        a = {(r, t): row_of(cols[t], r) for t in range(8) for r in range(t + 1)}
        opened = jnp.where(inside, jnp.where(lane - base == sub, 1.0, 0.0), here)
        rows = [row_of(opened, r) for r in range(8)]
        has_next = p + 1 < 16
        if has_next:
            next_cols = [lane_of(groups[p + 1], base + t) for t in range(8)]
            next_group = jnp.where(inside, 0.0, groups[p + 1])
        m, inv = {}, {}
        out = jnp.zeros((8, 128), F32)
        for s in range(8):
            inv[s] = 1.0 / a[s, s]
            out = jnp.where(sub == s, rows[s] * lax.rsqrt(a[s, s]), out)
            for t in range(s + 1, 8):
                m[s, t] = a[s, t] * inv[s]
                for u in range(t, 8):
                    a[t, u] = a[t, u] - m[s, t] * a[s, u]
            if has_next:
                next_group = next_group - (next_cols[s] * inv[s]) * rows[s]
            for t in range(s + 1, 8):
                rows[t] = rows[t] - m[s, t] * rows[s]
                if has_next:
                    next_cols[t] = next_cols[t] - m[s, t] * next_cols[s]
        done[p] = out
        if p + 2 < 16:
            back = [None] * 8
            for s in range(7, -1, -1):
                g = rows[s] * inv[s]
                for t in range(s + 1, 8):
                    g = g - m[s, t] * back[t]
                back[s] = g
            for i in range(p + 2, 16):
                v = jnp.where(inside, 0.0, groups[i])
                for t in range(8):
                    v = v - lane_of(groups[i], base + t) * back[t]
                groups[i] = v
        if has_next:
            groups[p + 1] = next_group
    return jnp.concatenate(done, axis=0)


def factor_kernel(g_ref, auxs_ref, inv_ref, a_ref):
    lane = lax.broadcasted_iota(jnp.int32, (8, 128), 1)
    sub = lax.broadcasted_iota(jnp.int32, (8, 128), 0)
    row = lax.broadcasted_iota(jnp.int32, (128, 128), 0)
    col = lax.broadcasted_iota(jnp.int32, (128, 128), 1)
    n, blocks = PANEL, PANEL // 128
    a_ref[...] = g_ref[:, 0:PANEL]
    for k in range(blocks):
        at_k = slice(128 * k, 128 * k + 128)
        damp = auxs_ref[k // 4, 1:2, 128 * (k % 4):128 * (k % 4) + 128]
        a_ref[at_k, at_k] = a_ref[at_k, at_k] + jnp.where(row == col, damp, 0.0)
    for k in range(blocks):
        kb = 128 * k
        groups = [a_ref[kb + 8 * i:kb + 8 * i + 8, kb:kb + 128] for i in range(16)]
        inverse = jnp.where(row >= col, factor_block(groups, lane, sub), 0.0)
        inv_ref[kb:kb + 128, kb:kb + 128] = inverse
        if kb + 128 < n:
            inv_ref[kb:kb + 128, kb + 128:n] = jnp.zeros((128, n - kb - 128), F32)
            upper = dot(inverse, a_ref[kb:kb + 128, kb + 128:n])
        if k:
            left = dot(inverse, a_ref[kb:kb + 128, :kb])
            inv_ref[kb:kb + 128, :kb] = left
        for i in range(k + 1, blocks):
            ib = 128 * i
            mine = upper[:, ib - kb - 128:ib - kb]
            a_ref[ib:ib + 128, ib:n] = a_ref[ib:ib + 128, ib:n] - dot_t(mine, upper[:, ib - kb - 128:], HI)
            if k:
                a_ref[ib:ib + 128, :kb] = a_ref[ib:ib + 128, :kb] - dot_t(mine, left, HI)
            a_ref[ib:ib + 128, kb:kb + 128] = -dot_t(mine, inverse, HI)


def factor(g, auxs):
    return pl.pallas_call(
        factor_kernel,
        out_shape=jax.ShapeDtypeStruct((PANEL, PANEL), F32),
        in_specs=[VM, VM],
        out_specs=VM,
        scratch_shapes=[pltpu.VMEM((PANEL, PANEL), F32)],
        compiler_params=params(),
        cost_estimate=pl.CostEstimate(flops=20 * 10**9, bytes_accessed=200 * 2**20, transcendentals=0),
        name="panel_factor",
    )(g, auxs)


def finish_kernel(inv_ref, g_ref, f_ref, e_ref, aux_ref, hess_ref, fac_ref, upd_ref, h1, u, u12):
    dp, z, h, x = spot()
    c, y = dp % 2, dp // 2
    first_col = (z * 8 + h * 4 + x) * 512
    damp = aux_ref[1:2, :]

    def damped(value, first_row):
        row = first_row + lax.broadcasted_iota(jnp.int32, value.shape, 0)
        col = first_col + lax.broadcasted_iota(jnp.int32, value.shape, 1)
        return value + jnp.where(row == col, damp, 0.0)

    mine = pl.multiple_of(512 * c, 512)
    theirs = pl.multiple_of(512 * (1 - c), 512)
    h1[pl.ds(mine, 512), :] = damped(f_ref[0:512, :], mine)
    h1[pl.ds(theirs, 512), :] = damped(e_ref[0:512, :], theirs)

    @pl.when(y == 0)
    def _():
        hess_ref[...] = h1[pl.ds(mine, 512), :]

    @pl.when(y == 1)
    def _():
        a = pl.multiple_of(256 * c, 256)
        b = pl.multiple_of(256 * (1 - c), 256)
        hess_ref[pl.ds(a, 256), :] = damped(f_ref[pl.ds(512 + a, 256), :], 1024 + 512 * c + a)
        hess_ref[pl.ds(b, 256), :] = damped(e_ref[512:768, :], 1024 + 512 * c + b)

    cols12 = pl.ds(pl.multiple_of(1024 + 256 * c, 256), 256)
    for k in range(8):
        rows = slice(128 * k, 128 * k + 128)
        left = inv_ref[rows, 0:128 * k + 128]
        u[rows, :] = dot(left, h1[0:128 * k + 128, :])
        u12[rows, :] = dot(left, g_ref[0:128 * k + 128, cols12])
    fac_ref[...] = u[pl.ds(pl.multiple_of(256 * dp, 256), 256), :]
    second = damped(f_ref[pl.ds(pl.multiple_of(512 + 256 * y, 256), 256), :], 1024 + 256 * dp)
    upd_ref[...] = second - dot_t(u12[...], u[...], HI)


def finish(inv, g, final, extra, aux):
    return pl.pallas_call(
        finish_kernel,
        out_shape=(
            jax.ShapeDtypeStruct((512, 512), F32),
            jax.ShapeDtypeStruct((256, 512), F32),
            jax.ShapeDtypeStruct((256, 512), F32),
        ),
        in_specs=[VM] * 5,
        out_specs=(VM, VM, VM),
        scratch_shapes=[
            pltpu.VMEM((1024, 512), F32),
            pltpu.VMEM((1024, 512), F32),
            pltpu.VMEM((1024, 256), F32),
        ],
        compiler_params=params(),
        name="finish_rows",
    )(inv, g, final, extra, aux)


def body(hidden_states, norm_gain, damping):
    aux = jnp.concatenate(
        [norm_gain.astype(F32)[None], damping[None], jnp.zeros((6, norm_gain.shape[0]), F32)], axis=0
    )
    w, auxs, ssq = spread(hidden_states, aux)
    slab, share = gram(w, auxs, ssq, hidden_states, aux)
    g, chip = join(slab, share)
    g = g.reshape(PANEL, 1536)
    far = lax.ppermute(chip, "dp", [(0, 2), (2, 0), (1, 3), (3, 1)])
    inv = factor(g, auxs)
    final = chip + far
    core = lax.axis_index("dp") % 2
    block = lax.dynamic_slice_in_dim(final, 512 + 256 * (1 - core), 256, 0)
    extra = lax.ppermute(
        jnp.concatenate([final[:512], block], axis=0), "dp", [(0, 1), (1, 0), (2, 3), (3, 2)]
    )
    return finish(inv, g, final, extra, aux)


def solution(mesh):
    return jax.shard_map(
        body,
        mesh=mesh,
        in_specs=(P("dp", "mp"), P("mp"), P("mp")),
        out_specs=(P("dp", "mp"), P("dp", "mp"), P("dp", "mp")),
        check_vma=False,
    )
```

time: 1480 us -> 244 us (0.16); the launches traced: 1460 us -> 240 us
  waiting for transfers between devices: 961 us -> 46.2 us
  other arithmetic: 270 us -> 4.22 us
  Pallas kernels: 0 us -> 184 us
  blocking collectives: 84.4 us -> 0 us
  matrix products: 60.4 us -> 0 us
  local copies, waits for them, and re-layouts: 61.2 us -> 2.45 us
  between operations: 19.7 us -> 0.95 us
    psum x4 -> x0, waiting for transfers between devices: 961 us -> none  [the longest x1 354 us: spread(): return lax.psum(kept, axis)]
    another operation x33 -> x0, other arithmetic: 257 us -> none  [the longest x30 172 us: body(): lower_factor = jnp.linalg.cholesky(diagonal_block)]
    pallas_call x0 -> x5, Pallas kernels: none -> 184 us  [the longest x1 56.5 us: spread(): pl.pallas_call(spread_kernel, out_shape=(jax.ShapeDtypeStruct((4, 1024, 5...]
    psum x1 -> x0, blocking collectives: 84.4 us -> none  [body(): ssq = lax.psum(jnp.sum(values * values, axis=1), 'mp')]
    another operation x29 -> x0, matrix products: 49 us -> none  [the longest x15 25.9 us: body(): lax.linalg.triangular_solve(lower_factor, column_slab[:PANEL], left_side=...]
    ppermute x0 -> x2, waiting for transfers between devices: none -> 46.2 us  [the longest x1 46.2 us: body(): far = lax.ppermute(chip, 'dp', [(0, 2), (2, 0), (1, 3), (3, 1)])]
    another operation x33 -> x0, local copies, waits for them, and re-layouts: 25.7 us -> none
  transfers between devices with their start and end apart: 4 -> 2, of which waited for: 4 -> 1; matrix products, arithmetic and copies ran while one was open for 0% -> 0% of each run, Pallas kernels for 0% -> 20%
where the time goes in v1:
time: 244 us; the launch traced here: 240 us
  Pallas kernels  184 us (75%)
  waiting for transfers between devices  46.2 us (19%)
  other arithmetic  4.22 us (2%)
  starting transfers between devices  2.62 us (1%)
  local copies, waits for them, and re-layouts  2.45 us (1%)
    pallas_call x1, Pallas kernels, spread(): pl.pallas_call(spread_kernel, out_shape=(jax.ShapeDtypeStruct((4, 1024, 5...  56.5 us
    pallas_call x1, Pallas kernels, join(): pl.pallas_call(join_kernel, out_shape=(jax.ShapeDtypeStruct((4, 4, 2, 32,...  52.3 us
    pallas_call x1, Pallas kernels, factor(): pl.pallas_call(factor_kernel, out_shape=jax.ShapeDtypeStruct((PANEL, PANE...  46.9 us
    ppermute x1, waiting for transfers between devices, body(): far = lax.ppermute(chip, 'dp', [(0, 2), (2, 0), (1, 3), (3, 1)])  46.2 us
    pallas_call x1, Pallas kernels, finish(): pl.pallas_call(finish_kernel, out_shape=(jax.ShapeDtypeStruct((512, 512),...  15.5 us
    pallas_call x1, Pallas kernels, gram(): pl.pallas_call(gram_kernel, out_shape=(jax.ShapeDtypeStruct((2048, 512),...  12.4 us
  transfers between devices with their start and end apart: 2, of which 1 were waited for; matrix products, arithmetic and copies ran while one was open for 0% of the time, Pallas kernels for 20%

profile of v1, /device:TPU:1, one launch (start us, length us, event | category | flops | bytes accessed | tf_op | source)
XLA Modules:
  0.0 240.1 jit_solution(16547178441014308336)
XLA Ops:
  0.6 0.7 broadcast_in_dim.16
  1.3 0.1 pad.4.clone
  1.4 1.4 maximum_maximum_fusion.aux_ref
  2.7 56.5 %spread_window.1 = (bf16[4,1024,512]{2,1,0:T(8,128)(2,1)}, f32[4,8,512]{2,1,0:T(8,128)}, f32[8,128]{1,0:T(8,128)}) custom-call(bf16[1024,512]{1,0:T(8,128)(2,1)} %x_ref.3, f32[8,512]{1,0:T(8,128)} %maximum_maximum_fusion.aux_ref), custom_call_target="tpu_custom_call" | custom-call | tf_op jit(solution)/shard_map/spread_window/pallas_call | solution.py:151
  59.3 12.4 %partial_gram.1 = (f32[2048,512]{1,0:T(8,128)}, f32[64,2048]{1,0:T(8,128)}) custom-call(bf16[4,1024,512]{2,1,0:T(8,128)(2,1)} %get-tuple-element.10.w_ref, f32[4,8,512]{2,1,0:T(8,128)} %get-tuple-element.11.auxs_ref, f32[8,128]{1,0:T(8,128)} %get-tuple-element.12.ssq_ref, bf16[1024,512]{1,0:T(8,128)(2,1)} %x_ref.3, f32[8,512]{1,0:T(8,128)} %maximum_maximum_fusion.aux_ref), custom_call_target="tpu_custom_call" | custom-call | tf_op jit(solution)/shard_map/partial_gram/pallas_call | solution.py:211
  71.7 52.3 %join_window.1 = (f32[4,4,2,32,1536]{4,3,2,1,0:T(8,128)}, f32[1024,512]{1,0:T(8,128)}) custom-call(f32[2048,512]{1,0:T(8,128)} %get-tuple-element.13.slab_ref, f32[64,2048]{1,0:T(8,128)} %get-tuple-element.14.share_ref), custom_call_target="tpu_custom_call" | custom-call | tf_op jit(solution)/shard_map/join_window/pallas_call | solution.py:302
  124.0 1.2 collective-permute-start
  125.2 46.2 %collective-permute-done = f32[1024,512]{1,0:T(8,128)S(1)} collective-permute-done((f32[1024,512]{1,0:T(8,128)}, f32[1024,512]{1,0:T(8,128)S(1)}, u32[]{:S(2)}, u32[]{:S(2)}) %collective-permute-start) | collective-permute-done | bytes 2097184 | tf_op jit(solution)/shard_map/ppermute | solution.py:486
  171.5 2.1 add.12.f_ref
  173.5 0.0 copy-start
  173.6 0.1 slice.4
  173.7 0.1 pad_maximum_fusion
  173.8 1.1 copy-done
  174.9 1.4 collective-permute-start.1
  176.3 46.9 %panel_factor.1.inv_ref = f32[1024,1024]{1,0:T(8,128)} custom-call(f32[1024,1536]{1,0:T(8,128)} %bitcast.3, f32[4,8,512]{2,1,0:T(8,128)} %get-tuple-element.11.auxs_ref), custom_call_target="tpu_custom_call" | custom-call | flops 20000000000 | bytes 209715200 | tf_op jit(solution)/shard_map/panel_factor/pallas_call | solution.py:408
  223.2 0.0 collective-permute-done.1.e_ref
  223.2 0.0 copy-start.1
  223.2 1.2 copy-done.1
  224.3 15.5 %finish_rows.1 = (f32[512,512]{1,0:T(8,128)}, f32[256,512]{1,0:T(8,128)}, f32[256,512]{1,0:T(8,128)}) custom-call(f32[1024,1024]{1,0:T(8,128)} %panel_factor.1.inv_ref, f32[1024,1536]{1,0:T(8,128)} %bitcast.4, f32[1024,512]{1,0:T(8,128)} %copy-done, f32[768,512]{1,0:T(8,128)} %copy-done.1, f32[8,512]{1,0:T(8,128)} %maximum_maximum_fusion.aux_ref), custom_call_target="tpu_custom_call" | custom-call | tf_op jit(solution)/shard_map/finish_rows/pallas_call | solution.py:459
  (2 shorter events, 0.0 us)
Async XLA Ops:
  124.0 47.5 %collective-permute-start = (f32[1024,512]{1,0:T(8,128)}, f32[1024,512]{1,0:T(8,128)S(1)}, u32[]{:S(2)}, u32[]{:S(2)}) collective-permute-start(f32[1024,512]{1,0:T(8,128)} %get-tuple-element.16), channel_id=1, source_target_pairs={{0,64},{64,0},{32,96},{96,32},{1,65},{65,1},{33,97},{97,33},{2,66}... | collective-permute-start | bytes 6291464 | tf_op jit(solution)/shard_map/ppermute | solution.py:486
  173.5 1.3 copy-start
  174.9 48.3 %collective-permute-start.1 = (f32[768,512]{1,0:T(8,128)S(1)}, f32[768,512]{1,0:T(8,128)S(1)}, u32[]{:S(2)}, u32[]{:S(2)}) collective-permute-start(f32[768,512]{1,0:T(8,128)S(1)} %pad_maximum_fusion), channel_id=1, source_target_pairs={{0,32},{32,0},{64,96},{96,64},{1,33},{33,1},{65,97},{97,65},{2,34}... | collective-permute-start | bytes 4718600 | tf_op jit(solution)/shard_map/ppermute | solution.py:491
  223.2 1.2 copy-start.1

commit v2 on v0

v2 whole, which is shorter than its diff:
```python
import functools

import jax
import jax.numpy as jnp
from jax import lax
from jax.experimental import pallas as pl
from jax.experimental.pallas import tpu as pltpu
from jax.sharding import PartitionSpec as P

D = 16384
PANEL = 1024
TOKENS = 4096
MESH = pl.DeviceIdType.MESH
HI = lax.Precision.HIGHEST
F32 = jnp.float32
BF16 = jnp.bfloat16
VM = pl.BlockSpec(memory_space=pltpu.VMEM)


def params(**kw):
    return pltpu.CompilerParams(vmem_limit_bytes=60 * 2**20, **kw)


def spot():
    mp = lax.axis_index("mp")
    return lax.axis_index("dp"), mp // 8, (mp // 4) % 2, mp % 4


def at(dp, z, h, x):
    return (dp, z * 8 + h * 4 + x)


def greet(partners):
    barrier = pltpu.get_barrier_semaphore()
    for p in partners:
        pl.semaphore_signal(barrier, inc=1, device_id=p, device_id_type=MESH)
    pl.semaphore_wait(barrier, len(partners))


def dot_t(a, b, precision=None):
    return lax.dot_general(a, b, (((0,), (0,)), ((), ())), precision=precision, preferred_element_type=F32)


def dot(a, b):
    return jnp.dot(a, b, precision=HI, preferred_element_type=F32)


def parts(v):
    a = v.astype(BF16)
    r = v - a.astype(F32)
    b = r.astype(BF16)
    return a, b, (r - b.astype(F32)).astype(BF16)


def left_of(p, axis):
    a, b, c = p
    return jnp.concatenate([a, a, a, b, b, c], axis=axis)


def right_of(p, axis):
    a, b, c = p
    return jnp.concatenate([a, b, c, a, b, a], axis=axis)


def dot6(a, b):
    return jnp.dot(left_of(parts(a), 1), right_of(parts(b), 0), preferred_element_type=F32)


def lane_of(v, j):
    return jnp.broadcast_to(v[:, j:j + 1], (8, 128))


def row_of(v, r):
    return jnp.broadcast_to(v[r:r + 1, :], (8, 128))


def factor_block(groups, lane, sub, hook):
    done = [None] * 16
    groups = list(groups)
    for p in range(16):
        base = 8 * p
        here = groups[p]
        inside = (lane >= base) & (lane < base + 8)
        cols = [lane_of(here, base + t) for t in range(8)]
        a = {(r, t): row_of(cols[t], r) for t in range(8) for r in range(t + 1)}
        opened = jnp.where(inside, jnp.where(lane - base == sub, 1.0, 0.0), here)
        rows = [row_of(opened, r) for r in range(8)]
        has_next = p + 1 < 16
        if has_next:
            next_cols = [lane_of(groups[p + 1], base + t) for t in range(8)]
            next_group = jnp.where(inside, 0.0, groups[p + 1])
        m, inv = {}, {}
        out = jnp.zeros((8, 128), F32)
        for s in range(8):
            inv[s] = 1.0 / a[s, s]
            out = jnp.where(sub == s, rows[s] * lax.rsqrt(a[s, s]), out)
            for t in range(s + 1, 8):
                m[s, t] = a[s, t] * inv[s]
                for u in range(t, 8):
                    a[t, u] = a[t, u] - m[s, t] * a[s, u]
            if has_next:
                next_group = next_group - (next_cols[s] * inv[s]) * rows[s]
            for t in range(s + 1, 8):
                rows[t] = rows[t] - m[s, t] * rows[s]
                if has_next:
                    next_cols[t] = next_cols[t] - m[s, t] * next_cols[s]
        done[p] = out
        if p + 2 < 16:
            back = [None] * 8
            for s in range(7, -1, -1):
                g = rows[s] * inv[s]
                for t in range(s + 1, 8):
                    g = g - m[s, t] * back[t]
                back[s] = g
            for i in range(p + 2, 16):
                v = jnp.where(inside, 0.0, groups[i])
                for t in range(8):
                    v = v - lane_of(groups[i], base + t) * back[t]
                groups[i] = v
        if has_next:
            groups[p + 1] = next_group
        hook(p)
    return jnp.concatenate(done, axis=0)


def factor_panel(a_ref, d_ref, xl_ref, xr_ref, li_ref, inv_ref, after):
    n, blocks = PANEL, PANEL // 128
    lane = lax.broadcasted_iota(jnp.int32, (8, 128), 1)
    sub = lax.broadcasted_iota(jnp.int32, (8, 128), 0)
    row = lax.broadcasted_iota(jnp.int32, (128, 128), 0)
    col = lax.broadcasted_iota(jnp.int32, (128, 128), 1)
    wide = lax.broadcasted_iota(jnp.int32, (128, n), 1)
    wide_row = lax.broadcasted_iota(jnp.int32, (128, n), 0)

    def rows_of(k):
        kb = pl.multiple_of(128 * k, 128)
        own = (wide >= kb) & (wide < kb + 128)
        r = jnp.where(own, jnp.where(wide - kb == wide_row, 1.0, 0.0), a_ref[pl.ds(kb, 128), :])
        v = dot6(li_ref[...], r)
        inv_ref[pl.ds(kb, 128), :] = jnp.where(wide < kb + 128, v, 0.0)
        return v

    d_ref[...] = a_ref[0:128, 0:128]
    li_ref[...] = jnp.zeros((128, 128), F32)

    def turn(k, carry):
        kb = pl.multiple_of(128 * k, 128)
        groups = [d_ref[8 * i:8 * i + 8, :] for i in range(16)]
        prev = jnp.maximum(k - 1, 0)
        pb = pl.multiple_of(128 * prev, 128)
        v = parts(rows_of(prev))
        xl_ref[...] = left_of(v, 0)
        xr_ref[...] = right_of(v, 0)
        gone = (wide >= pb) & (wide < pb + 128)

        def hook(p):
            if not 1 <= p <= 14:
                return
            i, half = 1 + (p - 1) // 2, (p - 1) % 2
            rows, cols = slice(128 * i, 128 * i + 128), slice(512 * half, 512 * half + 512)
            on = (i >= k) & (k > 0)
            old = a_ref[rows, cols]
            new = jnp.where(gone[:, cols], 0.0, old) - dot_t(xl_ref[:, rows], xr_ref[:, cols])
            a_ref[rows, cols] = jnp.where(on, new, old)

        li = jnp.where(row >= col, factor_block(groups, lane, sub, hook), 0.0)
        li_ref[...] = li
        nb = pl.multiple_of(128 * jnp.minimum(k + 1, blocks - 1), 128)
        v = parts(dot6(li, a_ref[pl.ds(kb, 128), pl.ds(nb, 128)]))
        d_ref[...] = a_ref[pl.ds(nb, 128), pl.ds(nb, 128)] - dot_t(left_of(v, 0), right_of(v, 0))
        after(k)
        return carry

    lax.fori_loop(0, blocks, turn, 0)
    rows_of(blocks - 1)


def main_kernel(x_ref, aux_ref, inv_ref, h12_ref, f_ref, e_ref,
                w, auxs, sx, sz, sh, wn, xn, rms, wide, share, share_in, share_sum, share_y, g,
                slab, other, chip, far, a, d, xl, xr, li, ss, rs):
    dp, z, h, x = spot()
    c, y = dp % 2, dp // 2
    column = [at(dp, (z + q // 2) % 4, (h + q % 2) % 2, x) for q in range(1, 8)]
    ring_x = [at(dp, z, h, (x + j) % 4) for j in range(1, 4)]
    ring_z = [at(dp, (z + j) % 4, h, x) for j in range(1, 4)]
    peer_h = at(dp, z, 1 - h, x)
    peer_c = at(y * 2 + 1 - c, z, h, x)
    peer_y = at((1 - y) * 2 + c, z, h, x)
    greet(column + ring_x + [peer_c, peer_y])
    sent = []

    def copy(src, dst, i, dev, to=None):
        k = pltpu.make_async_remote_copy(src_ref=src, dst_ref=dst, send_sem=ss.at[i],
                                         recv_sem=rs.at[i if to is None else to],
                                         device_id=dev, device_id_type=MESH)
        return k

    def start(copies):
        for k in copies:
            k.start()
            sent.append(k)

    def arrive(copies):
        for k in copies:
            k.wait_recv()

    is_source = (z == 0) & (h == 0)

    def scatter(q):
        b = (q // 2) * 128 + (q % 2) * 64
        dev = column[q - 1]
        return [
            copy(aux_ref, auxs.at[x], 3 * q, dev, 0),
            copy(x_ref.at[pl.ds(512 + b, 64)], w.at[x, pl.ds(512 + b, 64)], 3 * q + 1, dev, 1),
            copy(x_ref.at[pl.ds(b, 64)], w.at[x, pl.ds(b, 64)], 3 * q + 2, dev, 2),
        ]

    @pl.when(is_source)
    def _():
        for q in range(1, 8):
            for k in scatter(q):
                k.start()
        w[x, 0:64] = x_ref[0:64]
        w[x, 512:576] = x_ref[512:576]
        auxs[x] = aux_ref[...]

    part = jnp.zeros((1024, 128), F32)
    for i in range(4):
        v = x_ref[:, 128 * i:128 * i + 128].astype(F32)
        part = part + v * v
    line = jnp.sum(part.T, axis=0, keepdims=True)
    for i in range(8):
        sx[x, i:i + 1, :] = line[:, 128 * i:128 * i + 128]
    sum_x = [copy(sx.at[x], sx.at[x], 47 + j, ring_x[j]) for j in range(3)]
    start(sum_x)

    @pl.when(jnp.logical_not(is_source))
    def _():
        arrive(scatter(1))

    own = pl.multiple_of(z * 128 + h * 64, 64)
    own_a, own_b = w.at[x, pl.ds(own, 64)], w.at[x, pl.ds(512 + own, 64)]
    step_2b = [copy(own_b, own_b, 26 + q, column[q - 1]) for q in range(1, 8)]
    step_2a = [copy(own_a, own_a, 24 + j, ring_x[j]) for j in range(3)]
    step_aux = [copy(auxs.at[x], auxs.at[x], 34 + j, ring_x[j]) for j in range(3)]
    start(step_2a + step_2b + step_aux)
    arrive(sum_x)
    sz[z] = (sx[0] + sx[1]) + (sx[2] + sx[3])
    sum_z = [copy(sz.at[z], sz.at[z], 50 + j, ring_z[j]) for j in range(3)]
    start(sum_z)
    all_a, all_b = w.at[:, pl.ds(own, 64)], w.at[x, pl.ds(512, 512)]
    step_3a = [copy(all_a, all_a, 36 + q, column[q - 1]) for q in range(1, 8)]
    step_3b = [copy(all_b, all_b, 44 + j, ring_x[j]) for j in range(3)]
    arrive(step_2a)
    start(step_3a)
    arrive(step_2b)
    start(step_3b)
    arrive(sum_z)
    sh[h] = (sz[0] + sz[1]) + (sz[2] + sz[3])
    sum_h = [copy(sh.at[h], sh.at[h], 53, peer_h)]
    start(sum_h)
    arrive(sum_h)

    inverse = lax.rsqrt((sh[0] + sh[1]) / D + 1e-05)
    for i in range(8):
        rms[128 * i:128 * i + 128, :] = jnp.broadcast_to(inverse[i:i + 1, :], (128, 128)).T

    @pl.loop(0, 8)
    def _(i):
        rows = pl.ds(pl.multiple_of(i * 128, 128), 128)
        scale = jnp.concatenate([rms[rows, :]] * 4, axis=1)
        xn[rows, :] = (x_ref[rows, :].astype(F32) * scale * aux_ref[0:1, :]).astype(BF16)

    arrive(step_aux)
    arrive(step_3a)
    arrive(step_3b)

    @pl.loop(0, 8)
    def _(i):
        rows = pl.ds(pl.multiple_of(i * 128, 128), 128)
        scale = jnp.concatenate([rms[rows, :]] * 4, axis=1)
        for b in range(4):
            wn[b, rows, :] = (w[b, rows, :].astype(F32) * scale * auxs[b, 0:1, :]).astype(BF16)

    s = z * 4 + x
    strip = wn[s // 8, :, pl.ds(pl.multiple_of(((s % 8) // 2) * 128, 128), 128)]
    for b in range(4):
        wide[:, 512 * b:512 * b + 512] = dot_t(strip, wn[b]) * (1.0 / TOKENS)
    share[...] = wide[pl.ds(pl.multiple_of((s % 2) * 64, 64), 64), :]
    to_core = [copy(share.at[pl.ds(pl.multiple_of(32 * (1 - c), 32), 32)], share_in, 54, peer_c)]
    start(to_core)

    def slab_rows(lo, hi):
        @pl.loop(lo, hi)
        def _(i):
            left = wn[i // 4, :, pl.ds(pl.multiple_of((i % 4) * 128, 128), 128)]
            slab[pl.ds(pl.multiple_of(i * 128, 128), 128), :] = dot_t(left, xn[...]) * (1.0 / TOKENS)

    slab_rows(0, 4)
    arrive(to_core)
    share_sum[...] = share[pl.ds(pl.multiple_of(32 * c, 32), 32), :] + share_in[...]
    give = pl.ds(pl.multiple_of(1024 + 512 * (1 - y), 512), 512)
    keep = pl.ds(pl.multiple_of(1024 + 512 * y, 512), 512)
    to_y = [copy(share_sum.at[:, pl.ds(0, 1024)], share_y.at[:, pl.ds(0, 1024)], 55, peer_y)]
    to_y2 = [copy(share_sum.at[:, give], share_y.at[:, pl.ds(1024, 512)], 56, peer_y)]
    start(to_y + to_y2)
    slab_rows(4, 16)
    arrive(to_y)
    g[z, x, c] = share_sum[:, 0:1024] + share_y[:, 0:1024]
    first, second = pl.ds(0, 16), pl.ds(16, 16)

    def gather_1(ref, i):
        one_a, one_b = ref.at[z, x, c, first], ref.at[z, x, c, second]
        return ([copy(one_a, one_a, i + j, ring_x[j]) for j in range(3)],
                [copy(one_b, one_b, i + 3 + j, ring_z[j]) for j in range(3)])

    def gather_2(ref, i):
        row_a, row_b = ref.at[z, :, c, first], ref.at[:, x, c, second]
        return ([copy(row_a, row_a, i + j, ring_z[j]) for j in range(3)],
                [copy(row_b, row_b, i + 3 + j, ring_x[j]) for j in range(3)])

    g1, g2 = gather_1(g, 57), gather_2(g, 63)
    g_core = [copy(g.at[:, :, c, k], g.at[:, :, c, k], i, peer_c) for k, i in ((first, 69), (second, 70))]
    q1, q2 = gather_1(h12_ref, 75), gather_2(h12_ref, 81)
    q_core = [copy(h12_ref.at[:, :, c], h12_ref.at[:, :, c], 87, peer_c)]
    start(g1[0] + g1[1])
    spans = [(512 * (1 - c), 0, 512), (1024 + 256 * (1 - c), 512, 256), (1536 + 256 * (1 - c), 768, 256)]
    slabs = [
        copy(slab.at[pl.ds(pl.multiple_of(p, 256), n)], other.at[pl.ds(b, n)], 71 + i, peer_c)
        for i, (p, b, n) in enumerate(spans)
    ]
    start(slabs)
    arrive(g1[0])
    start(g2[0])
    arrive(g1[1])
    start(g2[1])
    arrive(to_y2)
    h12_ref[z, x, c] = share_sum[:, keep] + share_y[:, 1024:1536]
    arrive(slabs)
    chip[0:512, :] = slab[pl.ds(pl.multiple_of(512 * c, 512), 512), :] + other[0:512, :]
    chip[512:768, :] = slab[pl.ds(pl.multiple_of(1024 + 256 * c, 256), 256), :] + other[512:768, :]
    chip[768:1024, :] = slab[pl.ds(pl.multiple_of(1536 + 256 * c, 256), 256), :] + other[768:1024, :]
    slab_y = [copy(chip, far, 74, peer_y)]
    arrive(g2[0])
    start(g_core[:1])
    arrive(g2[1])
    start(g_core[1:])
    start(slab_y + q1[0] + q1[1])
    arrive(g_core)
    for i in range(4):
        for j in range(4):
            for k in range(2):
                lo = 64 * (4 * i + j) + 32 * k
                a[lo:lo + 32, :] = g[i, j, k]
    row = lax.broadcasted_iota(jnp.int32, (128, 128), 0)
    col = lax.broadcasted_iota(jnp.int32, (128, 128), 1)
    for k in range(8):
        at_k = slice(128 * k, 128 * k + 128)
        damp = auxs[k // 4, 1:2, 128 * (k % 4):128 * (k % 4) + 128]
        a[at_k, at_k] = a[at_k, at_k] + jnp.where(row == col, damp, 0.0)

    block = pl.multiple_of(512 + 256 * (1 - c), 256)
    to_e = [copy(f_ref.at[pl.ds(0, 512)], e_ref.at[pl.ds(0, 512)], 88, peer_c),
            copy(f_ref.at[pl.ds(block, 256)], e_ref.at[pl.ds(512, 256)], 89, peer_c)]

    def after(k):
        @pl.when(k == 1)
        def _():
            arrive(q1[0])
            arrive(q1[1])
            for m in q2[0] + q2[1]:
                m.start()

        @pl.when(k == 4)
        def _():
            arrive(q2[0])
            arrive(q2[1])
            for m in q_core:
                m.start()

        @pl.when(k == 6)
        def _():
            arrive(slab_y)
            f_ref[...] = chip[...] + far[...]
            for m in to_e:
                m.start()

    factor_panel(a, d, xl, xr, li, inv_ref, after)
    arrive(q_core + to_e)
    for k in sent + q2[0] + q2[1] + q_core + to_e:
        k.wait_send()

    @pl.when(is_source)
    def _():
        for q in range(1, 8):
            for k in scatter(q):
                k.wait_send()


def main(hidden, aux):
    def f32(*shape):
        return pltpu.VMEM(shape, F32)

    def b16(*shape):
        return pltpu.VMEM(shape, BF16)

    return pl.pallas_call(
        main_kernel,
        out_shape=(
            jax.ShapeDtypeStruct((PANEL, PANEL), F32),
            jax.ShapeDtypeStruct((4, 4, 2, 32, 512), F32),
            jax.ShapeDtypeStruct((1024, 512), F32),
            jax.ShapeDtypeStruct((768, 512), F32),
        ),
        in_specs=[VM, VM],
        out_specs=(VM, VM, VM, VM),
        scratch_shapes=[
            b16(4, 1024, 512), f32(4, 8, 512), f32(4, 8, 128), f32(4, 8, 128), f32(2, 8, 128),
            b16(4, 1024, 512), b16(1024, 512), f32(1024, 128), f32(128, 2048), f32(64, 2048),
            f32(32, 2048), f32(32, 2048), f32(32, 1536), f32(4, 4, 2, 32, 1024),
            f32(2048, 512), f32(1024, 512), f32(1024, 512), f32(1024, 512),
            f32(PANEL, PANEL), f32(128, 128), b16(768, PANEL), b16(768, PANEL), f32(128, 128),
            pltpu.SemaphoreType.DMA((90,)),
            pltpu.SemaphoreType.DMA((90,)),
        ],
        compiler_params=params(collective_id=0, has_side_effects=True),
        name="window_panel",
    )(hidden, aux)


def finish_kernel(inv_ref, g_ref, f_ref, e_ref, aux_ref, hess_ref, fac_ref, upd_ref, h1, u, u12):
    dp, z, h, x = spot()
    c, y = dp % 2, dp // 2
    first_col = (z * 8 + h * 4 + x) * 512
    damp = aux_ref[1:2, :]

    def damped(value, first_row):
        row = first_row + lax.broadcasted_iota(jnp.int32, value.shape, 0)
        col = first_col + lax.broadcasted_iota(jnp.int32, value.shape, 1)
        return value + jnp.where(row == col, damp, 0.0)

    mine = pl.multiple_of(512 * c, 512)
    theirs = pl.multiple_of(512 * (1 - c), 512)
    h1[pl.ds(mine, 512), :] = damped(f_ref[0:512, :], mine)
    h1[pl.ds(theirs, 512), :] = damped(e_ref[0:512, :], theirs)

    @pl.when(y == 0)
    def _():
        hess_ref[...] = h1[pl.ds(mine, 512), :]

    @pl.when(y == 1)
    def _():
        a = pl.multiple_of(256 * c, 256)
        b = pl.multiple_of(256 * (1 - c), 256)
        hess_ref[pl.ds(a, 256), :] = damped(f_ref[pl.ds(512 + a, 256), :], 1024 + 512 * c + a)
        hess_ref[pl.ds(b, 256), :] = damped(e_ref[512:768, :], 1024 + 512 * c + b)

    cols12 = pl.ds(pl.multiple_of(256 * c, 256), 256)
    for k in range(8):
        rows = slice(128 * k, 128 * k + 128)
        left = inv_ref[rows, 0:128 * k + 128]
        u[rows, :] = dot(left, h1[0:128 * k + 128, :])
        u12[rows, :] = dot(left, g_ref[0:128 * k + 128, cols12])
    fac_ref[...] = u[pl.ds(pl.multiple_of(256 * dp, 256), 256), :]
    second = damped(f_ref[pl.ds(pl.multiple_of(512 + 256 * y, 256), 256), :], 1024 + 256 * dp)
    upd_ref[...] = second - dot_t(u12[...], u[...], HI)


def finish(inv, g, final, extra, aux):
    return pl.pallas_call(
        finish_kernel,
        out_shape=(
            jax.ShapeDtypeStruct((512, 512), F32),
            jax.ShapeDtypeStruct((256, 512), F32),
            jax.ShapeDtypeStruct((256, 512), F32),
        ),
        in_specs=[VM] * 5,
        out_specs=(VM, VM, VM),
        scratch_shapes=[
            pltpu.VMEM((1024, 512), F32),
            pltpu.VMEM((1024, 512), F32),
            pltpu.VMEM((1024, 256), F32),
        ],
        compiler_params=params(),
        name="finish_rows",
    )(inv, g, final, extra, aux)


def body(hidden_states, norm_gain, damping):
    aux = jnp.concatenate(
        [norm_gain.astype(F32)[None], damping[None], jnp.zeros((6, norm_gain.shape[0]), F32)], axis=0
    )
    inv, h12, final, extra = main(hidden_states, aux)
    return finish(inv, h12.reshape(PANEL, 512), final, extra, aux)


def solution(mesh):
    return jax.shard_map(
        body,
        mesh=mesh,
        in_specs=(P("dp", "mp"), P("mp"), P("mp")),
        out_specs=(P("dp", "mp"), P("dp", "mp"), P("dp", "mp")),
        check_vma=False,
    )
```

time: 1480 us -> 158 us (0.11); the launches traced: 1460 us -> 157 us
  waiting for transfers between devices: 961 us -> 0 us
  other arithmetic: 270 us -> 2.03 us
  Pallas kernels: 0 us -> 155 us
  blocking collectives: 84.4 us -> 0 us
  local copies, waits for them, and re-layouts: 61.2 us -> 0.08 us
  matrix products: 60.4 us -> 0 us
  between operations: 19.7 us -> 0.65 us
    psum x4 -> x0, waiting for transfers between devices: 961 us -> none  [the longest x1 354 us: spread(): return lax.psum(kept, axis)]
    another operation x33 -> x0, other arithmetic: 257 us -> none  [the longest x30 172 us: body(): lower_factor = jnp.linalg.cholesky(diagonal_block)]
    pallas_call x0 -> x2, Pallas kernels: none -> 155 us  [the longest x1 140 us: main(): pl.pallas_call(main_kernel, out_shape=(jax.ShapeDtypeStruct((PANEL, PANEL...]
    psum x1 -> x0, blocking collectives: 84.4 us -> none  [body(): ssq = lax.psum(jnp.sum(values * values, axis=1), 'mp')]
    another operation x29 -> x0, matrix products: 49 us -> none  [the longest x15 25.9 us: body(): lax.linalg.triangular_solve(lower_factor, column_slab[:PANEL], left_side=...]
    another operation x33 -> x0, local copies, waits for them, and re-layouts: 25.7 us -> none
  transfers between devices with their start and end apart: 4 -> 0, of which waited for: 4 -> 0; matrix products, arithmetic and copies ran while one was open for 0% -> 0% of each run, Pallas kernels for 0% -> 0%
where the time goes in v2:
time: 158 us; the launch traced here: 157 us
  Pallas kernels  155 us (98%)
  other arithmetic  2.03 us (1%)
    pallas_call x1, Pallas kernels, main(): pl.pallas_call(main_kernel, out_shape=(jax.ShapeDtypeStruct((PANEL, PANEL...  140 us
    pallas_call x1, Pallas kernels, finish(): pl.pallas_call(finish_kernel, out_shape=(jax.ShapeDtypeStruct((512, 512),...  14.3 us

profile of v2, /device:TPU:1, one launch (start us, length us, event | category | flops | bytes accessed | tf_op | source)
XLA Modules:
  0.0 157.3 jit_solution(18444427857161695158)
XLA Ops:
  0.6 0.1 pad.2.clone
  0.7 0.7 broadcast_in_dim.16
  1.4 1.3 maximum_maximum_fusion.aux_ref
  2.7 140.2 %window_panel.1 = (f32[1024,1024]{1,0:T(8,128)}, f32[4,4,2,32,512]{4,3,2,1,0:T(8,128)}, f32[1024,512]{1,0:T(8,128)}, f32[768,512]{1,0:T(8,128)}) custom-call(bf16[1024,512]{1,0:T(8,128)(2,1)} %x_ref.1, f32[8,512]{1,0:T(8,128)} %maximum_maximum_fusion.aux_ref), custom_call_target="tpu_custom_call" | custom-call | tf_op jit(solution)/shard_map/window_panel/pallas_call | solution.py:407
  143.0 14.3 %finish_rows.1 = (f32[512,512]{1,0:T(8,128)}, f32[256,512]{1,0:T(8,128)}, f32[256,512]{1,0:T(8,128)}) custom-call(f32[1024,1024]{1,0:T(8,128)} %get-tuple-element.7.inv_ref, f32[1024,512]{1,0:T(8,128)} %bitcast.3, f32[1024,512]{1,0:T(8,128)} %get-tuple-element.9.f_ref, f32[768,512]{1,0:T(8,128)} %get-tuple-element.10.e_ref, f32[8,512]{1,0:T(8,128)} %maximum_maximum_fusion.aux_ref), custom_call_target="tpu_custom_call" | custom-call | tf_op jit(solution)/shard_map/finish_rows/pallas_call | solution.py:470
  (1 shorter events, 0.0 us)

commit v3 on v2

v3 whole, which is shorter than its diff:
```python
import jax
import jax.numpy as jnp
from jax import lax
from jax.experimental import pallas as pl
from jax.experimental.pallas import tpu as pltpu
from jax.sharding import PartitionSpec as P

D = 16384
PANEL = 1024
TOKENS = 4096
MESH = pl.DeviceIdType.MESH
F32 = jnp.float32
BF16 = jnp.bfloat16
VM = pl.BlockSpec(memory_space=pltpu.VMEM)


def params(**kw):
    return pltpu.CompilerParams(vmem_limit_bytes=60 * 2**20, **kw)


def spot():
    mp = lax.axis_index("mp")
    return lax.axis_index("dp"), mp // 8, (mp // 4) % 2, mp % 4


def at(dp, z, h, x):
    return (dp, z * 8 + h * 4 + x)


def greet_signal(partners):
    barrier = pltpu.get_barrier_semaphore()
    for p in partners:
        pl.semaphore_signal(barrier, inc=1, device_id=p, device_id_type=MESH)


def greet_wait(count):
    pl.semaphore_wait(pltpu.get_barrier_semaphore(), count)


def dot_t(a, b):
    return lax.dot_general(a, b, (((0,), (0,)), ((), ())), preferred_element_type=F32)


def parts(v):
    a = v.astype(BF16)
    r = v - a.astype(F32)
    b = r.astype(BF16)
    return a, b, (r - b.astype(F32)).astype(BF16)


def whole_parts(v):
    v = jnp.concatenate([v, jnp.zeros_like(v)], axis=0)
    return parts(v)


def left_of(p, axis):
    a, b, c = p
    return jnp.concatenate([a, a, a, b, b, c], axis=axis)


def right_of(p, axis):
    a, b, c = p
    return jnp.concatenate([a, b, c, a, b, a], axis=axis)


def two_parts(v):
    a = v.astype(BF16)
    return a, (v - a.astype(F32)).astype(BF16)


def dot6(a, b):
    return jnp.dot(left_of(parts(a), 1), right_of(parts(b), 0), preferred_element_type=F32)


def lane_of(v, j):
    return jnp.broadcast_to(v[:, j:j + 1], (8, 128))


def row_of(v, r):
    return jnp.broadcast_to(v[r:r + 1, :], (8, 128))


def factor_block(groups, lane, sub, hook):
    done = [None] * 16
    groups = list(groups)
    for p in range(16):
        base = 8 * p
        here = groups[p]
        inside = (lane >= base) & (lane < base + 8)
        cols = [lane_of(here, base + t) for t in range(8)]
        a = {(r, t): row_of(cols[t], r) for t in range(8) for r in range(t + 1)}
        opened = jnp.where(inside, jnp.where(lane - base == sub, 1.0, 0.0), here)
        rows = [row_of(opened, r) for r in range(8)]
        has_next = p + 1 < 16
        if has_next:
            next_cols = [lane_of(groups[p + 1], base + t) for t in range(8)]
            next_group = jnp.where(inside, 0.0, groups[p + 1])
        m, inv = {}, {}
        out = jnp.zeros((8, 128), F32)
        for s in range(8):
            inv[s] = 1.0 / a[s, s]
            out = jnp.where(sub == s, rows[s] * lax.rsqrt(a[s, s]), out)
            for t in range(s + 1, 8):
                m[s, t] = a[s, t] * inv[s]
                for u in range(t, 8):
                    a[t, u] = a[t, u] - m[s, t] * a[s, u]
            if has_next:
                next_group = next_group - (next_cols[s] * inv[s]) * rows[s]
            for t in range(s + 1, 8):
                rows[t] = rows[t] - m[s, t] * rows[s]
                if has_next:
                    next_cols[t] = next_cols[t] - m[s, t] * next_cols[s]
        done[p] = out
        if p + 2 < 16:
            v = whole_parts(out)
            product = dot_t(left_of(v, 0), right_of(v, 0))
            for i in range(p + 2, 16):
                groups[i] = jnp.where(inside, 0.0, groups[i]) - product[8 * i:8 * i + 8, :]
        if has_next:
            groups[p + 1] = next_group
        hook(p)
    return jnp.concatenate(done, axis=0)


def factor_panel(a_ref, d_ref, xl_ref, xr_ref, li_ref, inv_ref, after):
    n, blocks = PANEL, PANEL // 128
    lane = lax.broadcasted_iota(jnp.int32, (8, 128), 1)
    sub = lax.broadcasted_iota(jnp.int32, (8, 128), 0)
    row = lax.broadcasted_iota(jnp.int32, (128, 128), 0)
    col = lax.broadcasted_iota(jnp.int32, (128, 128), 1)
    wide = lax.broadcasted_iota(jnp.int32, (128, n), 1)
    wide_row = lax.broadcasted_iota(jnp.int32, (128, n), 0)

    def rows_of(k):
        kb = pl.multiple_of(128 * k, 128)
        own = (wide >= kb) & (wide < kb + 128)
        r = jnp.where(own, jnp.where(wide - kb == wide_row, 1.0, 0.0), a_ref[pl.ds(kb, 128), :])
        v = dot6(li_ref[...], r)
        inv_ref[pl.ds(kb, 128), :] = jnp.where(wide < kb + 128, v, 0.0)
        return v

    d_ref[...] = a_ref[0:128, 0:128]
    li_ref[...] = jnp.zeros((128, 128), F32)

    def turn(k, carry):
        kb = pl.multiple_of(128 * k, 128)
        groups = [d_ref[8 * i:8 * i + 8, :] for i in range(16)]
        prev = jnp.maximum(k - 1, 0)
        pb = pl.multiple_of(128 * prev, 128)
        v = rows_of(prev)
        xl_ref[...] = left_of(parts(v.T), 1)
        xr_ref[...] = right_of(parts(v), 0)

        def hook(p):
            if not 1 <= p <= 8:
                return
            top, first = 128 + 448 * ((p - 1) % 2), 256 * ((p - 1) // 2)
            rows, cols = slice(top, top + 448), slice(first, first + 256)
            below = (top + lax.broadcasted_iota(jnp.int32, (448, 256), 0) >= kb) & (k > 0)
            at_col = first + lax.broadcasted_iota(jnp.int32, (448, 256), 1)
            gone = (at_col >= pb) & (at_col < pb + 128)
            old = a_ref[rows, cols]
            new = jnp.where(gone, 0.0, old) - jnp.dot(
                xl_ref[rows, :], xr_ref[:, cols], preferred_element_type=F32
            )
            a_ref[rows, cols] = jnp.where(below, new, old)

        li = jnp.where(row >= col, factor_block(groups, lane, sub, hook), 0.0)
        li_ref[...] = li
        nb = pl.multiple_of(128 * jnp.minimum(k + 1, blocks - 1), 128)
        v = parts(dot6(li, a_ref[pl.ds(kb, 128), pl.ds(nb, 128)]))
        d_ref[...] = a_ref[pl.ds(nb, 128), pl.ds(nb, 128)] - dot_t(left_of(v, 0), right_of(v, 0))
        after(k)
        return carry

    lax.fori_loop(0, blocks, turn, 0)
    rows_of(blocks - 1)


def main_kernel(x_ref, aux_ref, hess_ref, fac_ref, upd_ref,
                xs, w, auxs, sx, sz, wn, xn, rms, wide, share, share_in, share_sum, share_y, g,
                slab, other, chip, far, a, d, xl, xr, li, inv, h12, final, extra, h1, hp, hq, u, ss, rs):
    dp, z, h, x = spot()
    c, y = dp % 2, dp // 2
    column = [at(dp, (z + q // 2) % 4, (h + q % 2) % 2, x) for q in range(1, 8)]
    ring_x = [at(dp, z, h, (x + j) % 4) for j in range(1, 4)]
    ring_z = [at(dp, (z + j) % 4, h, x) for j in range(1, 4)]
    peer_c = at(y * 2 + 1 - c, z, h, x)
    peer_y = at((1 - y) * 2 + c, z, h, x)
    greet_signal(column + ring_x + [peer_c, peer_y])
    sent = []

    def copy(src, dst, i, dev, to=None):
        k = pltpu.make_async_remote_copy(src_ref=src, dst_ref=dst, send_sem=ss.at[i],
                                         recv_sem=rs.at[i if to is None else to],
                                         device_id=dev, device_id_type=MESH)
        return k

    def start(copies):
        for k in copies:
            k.start()
            sent.append(k)

    def arrive(copies):
        for k in copies:
            k.wait_recv()

    part = jnp.zeros((1024, 128), F32)
    for i in range(4):
        v = x_ref[:, 128 * i:128 * i + 128].astype(F32)
        part = part + v * v
    line = jnp.sum(part.T, axis=0, keepdims=True)
    for i in range(8):
        sx[x, i:i + 1, :] = line[:, 128 * i:128 * i + 128]
    is_source = (z == 0) & (h == 0)

    @pl.when(is_source)
    def _():
        own_damp = [v.astype(F32) for v in parts(aux_ref[1:2, :])]
        extra_rows = jnp.concatenate([aux_ref[0:1, :]] + own_damp + [jnp.zeros((12, 512), F32)], axis=0)
        for q in range(8):
            xs[q, 0:16, :] = extra_rows.astype(BF16)
            xs[q, 16:144, :] = x_ref[128 * q:128 * q + 128, :]
        w[x, 0] = xs[0]

    greet_wait(12)
    sum_x = [copy(sx.at[x], sx.at[x], 47 + j, ring_x[j]) for j in range(3)]
    start(sum_x)

    def scatter(q):
        return copy(xs.at[q], w.at[x, q], q, column[q - 1], 0)

    @pl.when(is_source)
    def _():
        for q in range(1, 8):
            scatter(q).start()

    own = z * 2 + h

    @pl.when(jnp.logical_not(is_source))
    def _():
        copy(xs.at[0], w.at[x, own], 0, column[0], 0).wait_recv()

    own_a, own_b = w.at[x, own, pl.ds(0, 80)], w.at[x, own, pl.ds(80, 64)]
    step_2b = [copy(own_b, own_b, 26 + q, column[q - 1]) for q in range(1, 8)]
    step_2a = [copy(own_a, own_a, 24 + j, ring_x[j]) for j in range(3)]
    start(step_2a + step_2b)
    arrive(sum_x)
    sz[own] = (sx[0] + sx[1]) + (sx[2] + sx[3])
    sum_c = [copy(sz.at[own], sz.at[own], 91 + q, column[q - 1]) for q in range(1, 8)]
    start(sum_c)
    all_a, all_b = w.at[:, own, pl.ds(16, 64)], w.at[x, :, pl.ds(80, 64)]
    step_3a = [copy(all_a, all_a, 36 + q, column[q - 1]) for q in range(1, 8)]
    step_3b = [copy(all_b, all_b, 44 + j, ring_x[j]) for j in range(3)]
    arrive(step_2a)
    start(step_3a)
    arrive(step_2b)
    start(step_3b)
    arrive(sum_c)

    total = ((sz[0] + sz[1]) + (sz[2] + sz[3])) + ((sz[4] + sz[5]) + (sz[6] + sz[7]))
    inverse = lax.rsqrt(total / D + 1e-05)
    for i in range(8):
        rms[128 * i:128 * i + 128, :] = jnp.broadcast_to(inverse[i:i + 1, :], (128, 128)).T

    @pl.loop(0, 8)
    def _(i):
        rows = pl.ds(pl.multiple_of(i * 128, 128), 128)
        scale = jnp.concatenate([rms[rows, :]] * 4, axis=1)
        xn[rows, :] = (x_ref[rows, :].astype(F32) * scale * aux_ref[0:1, :]).astype(BF16)

    for b in range(4):
        v = w[b, own, 0:16, :].astype(F32)
        auxs[b, 0:1, :] = v[0:1, :]
        auxs[b, 1:2, :] = (v[1:2, :] + v[2:3, :]) + v[3:4, :]
    arrive(step_3a)
    arrive(step_3b)

    def normalise(blocks):
        @pl.loop(0, 8)
        def _(i):
            rows = pl.ds(pl.multiple_of(i * 128, 128), 128)
            scale = jnp.concatenate([rms[rows, :]] * 4, axis=1)
            for b in blocks:
                wn[b, rows, :] = (w[b, i, 16:144, :].astype(F32) * scale * auxs[b, 0:1, :]).astype(BF16)

    s = z * 4 + x
    half = pl.ds(pl.multiple_of((s % 2) * 64, 64), 64)
    panels = [pl.ds(0, 1024), pl.ds(1024, 1024)]
    give, keep = pl.ds(pl.multiple_of(32 * (1 - c), 32), 32), pl.ds(pl.multiple_of(32 * c, 32), 32)

    def share_of(m):
        strip = wn[s // 8, :, pl.ds(pl.multiple_of(((s % 8) // 2) * 128, 128), 128)]
        for b in range(2):
            wide[:, 512 * b:512 * b + 512] = dot_t(strip, wn[2 * m + b]) * (1.0 / TOKENS)
        share[:, panels[m]] = wide[half, :]
        k = copy(share.at[give, panels[m]], share_in.at[:, panels[m]], 54 + 36 * m, peer_c)
        start([k])
        return k

    def slab_rows(b):
        slab[512 * b:512 * b + 512, :] = dot_t(wn[b], xn[...]) * (1.0 / TOKENS)

    normalise((0, 1))
    core_1 = share_of(0)
    normalise((2, 3))
    arrive([core_1])
    share_sum[:, panels[0]] = share[keep, panels[0]] + share_in[:, panels[0]]
    to_y = [copy(share_sum.at[:, panels[0]], share_y.at[:, pl.ds(0, 1024)], 55, peer_y)]
    start(to_y)
    core_2 = share_of(1)
    slab_rows(0)
    arrive(to_y)
    g[z, x, c] = share_sum[:, 0:1024] + share_y[:, 0:1024]
    first, second = pl.ds(0, 16), pl.ds(16, 16)

    def gather_1(ref, i):
        one_a, one_b = ref.at[z, x, c, first], ref.at[z, x, c, second]
        return ([copy(one_a, one_a, i + j, ring_x[j]) for j in range(3)],
                [copy(one_b, one_b, i + 3 + j, ring_z[j]) for j in range(3)])

    def gather_2(ref, i):
        row_a, row_b = ref.at[z, :, c, first], ref.at[:, x, c, second]
        return ([copy(row_a, row_a, i + j, ring_z[j]) for j in range(3)],
                [copy(row_b, row_b, i + 3 + j, ring_x[j]) for j in range(3)])

    g1, g2 = gather_1(g, 57), gather_2(g, 63)
    g_core = [copy(g.at[:, :, c, k], g.at[:, :, c, k], i, peer_c) for k, i in ((first, 69), (second, 70))]
    q1, q2 = gather_1(h12, 75), gather_2(h12, 81)
    q_core = [copy(h12.at[:, :, c], h12.at[:, :, c], 87, peer_c)]
    start(g1[0] + g1[1])
    arrive([core_2])
    share_sum[:, panels[1]] = share[keep, panels[1]] + share_in[:, panels[1]]
    far_12 = pl.ds(pl.multiple_of(1024 + 512 * (1 - y), 512), 512)
    near_12 = pl.ds(pl.multiple_of(1024 + 512 * y, 512), 512)
    to_y2 = [copy(share_sum.at[:, far_12], share_y.at[:, pl.ds(1024, 512)], 56, peer_y)]
    start(to_y2)
    slab_rows(1)
    spans = [(512 * (1 - c), 0, 512), (1024 + 256 * (1 - c), 512, 256), (1536 + 256 * (1 - c), 768, 256)]
    slabs = [
        copy(slab.at[pl.ds(pl.multiple_of(p, 256), n)], other.at[pl.ds(b, n)], 71 + i, peer_c)
        for i, (p, b, n) in enumerate(spans)
    ]
    start(slabs[:1])
    slab_y = [copy(chip.at[pl.ds(p, 512)], far.at[pl.ds(p, 512)], 73 + i, peer_y)
              for i, p in ((1, 0), (18, 512))]
    arrive(g1[0])
    start(g2[0])
    arrive(g1[1])
    start(g2[1])
    slab_rows(2)
    slab_rows(3)
    start(slabs[1:])
    arrive(to_y2)
    h12[z, x, c] = share_sum[:, near_12] + share_y[:, 1024:1536]
    arrive(slabs[:1])
    chip[0:512, :] = slab[pl.ds(pl.multiple_of(512 * c, 512), 512), :] + other[0:512, :]
    start(slab_y[:1])
    arrive(slabs[1:])
    chip[512:768, :] = slab[pl.ds(pl.multiple_of(1024 + 256 * c, 256), 256), :] + other[512:768, :]
    chip[768:1024, :] = slab[pl.ds(pl.multiple_of(1536 + 256 * c, 256), 256), :] + other[768:1024, :]
    start(slab_y[1:])
    arrive(g2[0])
    start(g_core[:1])
    arrive(g2[1])
    start(g_core[1:])
    start(q1[0] + q1[1])
    arrive(g_core)
    for i in range(4):
        for j in range(4):
            for k in range(2):
                lo = 64 * (4 * i + j) + 32 * k
                a[lo:lo + 32, :] = g[i, j, k]
    row = lax.broadcasted_iota(jnp.int32, (128, 128), 0)
    col = lax.broadcasted_iota(jnp.int32, (128, 128), 1)
    for k in range(8):
        at_k = slice(128 * k, 128 * k + 128)
        damp = auxs[k // 4, 1:2, 128 * (k % 4):128 * (k % 4) + 128]
        a[at_k, at_k] = a[at_k, at_k] + jnp.where(row == col, damp, 0.0)

    block = pl.multiple_of(512 + 256 * (1 - c), 256)
    to_e = [copy(final.at[pl.ds(0, 512)], extra.at[pl.ds(0, 512)], 88, peer_c),
            copy(final.at[pl.ds(block, 256)], extra.at[pl.ds(512, 256)], 89, peer_c)]

    def after(k):
        @pl.when(k == 1)
        def _():
            arrive(q1[0])
            arrive(q1[1])
            for m in q2[0] + q2[1]:
                m.start()

        @pl.when(k == 4)
        def _():
            arrive(q2[0])
            arrive(q2[1])
            for m in q_core:
                m.start()

        @pl.when(k == 5)
        def _():
            arrive(slab_y)
            final[...] = chip[...] + far[...]
            for m in to_e:
                m.start()

    factor_panel(a, d, xl, xr, li, inv, after)
    arrive(q_core + to_e)

    first_col = (z * 8 + h * 4 + x) * 512
    damp_own = aux_ref[1:2, :]

    def damped(value, first_row):
        rows = first_row + lax.broadcasted_iota(jnp.int32, value.shape, 0)
        cols = first_col + lax.broadcasted_iota(jnp.int32, value.shape, 1)
        return value + jnp.where(rows == cols, damp_own, 0.0)

    mine = pl.multiple_of(512 * c, 512)
    theirs = pl.multiple_of(512 * (1 - c), 512)
    h1[pl.ds(mine, 512), :] = damped(final[0:512, :], mine)
    h1[pl.ds(theirs, 512), :] = damped(extra[0:512, :], theirs)

    @pl.when(y == 0)
    def _():
        hess_ref[...] = h1[pl.ds(mine, 512), :]

    @pl.when(y == 1)
    def _():
        p = pl.multiple_of(256 * c, 256)
        q = pl.multiple_of(256 * (1 - c), 256)
        hess_ref[pl.ds(p, 256), :] = damped(final[pl.ds(512 + p, 256), :], 1024 + 512 * c + p)
        hess_ref[pl.ds(q, 256), :] = damped(extra[512:768, :], 1024 + 512 * c + q)

    for i in range(8):
        rows = slice(128 * i, 128 * i + 128)
        hp[rows, 0:512], hq[rows, 0:512] = two_parts(h1[rows, :])
        for j in range(2):
            p = 128 * i + 64 * j
            block12 = jnp.concatenate(
                [h12[i // 2, 2 * (i % 2) + j, m, :, pl.ds(pl.multiple_of(256 * c, 256), 256)] for m in range(2)], axis=0
            )
            hp[p:p + 64, 512:768], hq[p:p + 64, 512:768] = two_parts(block12)
    for i in range(2):
        rows, n = slice(512 * i, 512 * i + 512), 512 * i + 512
        p, q = two_parts(inv[rows, 0:n])
        u[rows, :] = jnp.dot(
            jnp.concatenate([p, p, q], axis=1),
            jnp.concatenate([hp[0:n, :], hq[0:n, :], hp[0:n, :]], axis=0),
            preferred_element_type=F32,
        )
    fac_ref[...] = u[pl.ds(pl.multiple_of(256 * dp, 256), 256), 0:512]
    p, q = two_parts(u[:, 512:768])
    v, r = two_parts(u[:, 0:512])
    upd_ref[...] = damped(
        final[pl.ds(pl.multiple_of(512 + 256 * y, 256), 256), :], 1024 + 256 * dp
    ) - dot_t(jnp.concatenate([p, p, q], axis=0), jnp.concatenate([v, r, v], axis=0))
    for k in sent + q2[0] + q2[1] + q_core + to_e:
        k.wait_send()

    @pl.when(is_source)
    def _():
        for q in range(1, 8):
            scatter(q).wait_send()


def main(hidden, aux):
    def f32(*shape):
        return pltpu.VMEM(shape, F32)

    def b16(*shape):
        return pltpu.VMEM(shape, BF16)

    return pl.pallas_call(
        main_kernel,
        out_shape=(
            jax.ShapeDtypeStruct((512, 512), F32),
            jax.ShapeDtypeStruct((256, 512), F32),
            jax.ShapeDtypeStruct((256, 512), F32),
        ),
        in_specs=[VM, VM],
        out_specs=(VM, VM, VM),
        scratch_shapes=[
            b16(8, 144, 512), b16(4, 8, 144, 512), f32(4, 8, 512), f32(4, 8, 128), f32(8, 8, 128),
            b16(4, 1024, 512), b16(1024, 512), f32(1024, 128), f32(128, 1024), f32(64, 2048),
            f32(32, 2048), f32(32, 2048), f32(32, 1536), f32(4, 4, 2, 32, 1024),
            f32(2048, 512), f32(1024, 512), f32(1024, 512), f32(1024, 512),
            f32(PANEL, PANEL), f32(128, 128), b16(PANEL, 768), b16(768, PANEL), f32(128, 128),
            f32(PANEL, PANEL), f32(4, 4, 2, 32, 512), f32(1024, 512), f32(768, 512),
            f32(1024, 512), b16(1024, 768), b16(1024, 768), f32(1024, 768),
            pltpu.SemaphoreType.DMA((100,)),
            pltpu.SemaphoreType.DMA((100,)),
        ],
        compiler_params=params(collective_id=0, has_side_effects=True),
        name="window_panel",
    )(hidden, aux)


def body(hidden_states, norm_gain, damping):
    aux = jnp.concatenate(
        [norm_gain.astype(F32)[None], damping[None], jnp.zeros((6, norm_gain.shape[0]), F32)], axis=0
    )
    return main(hidden_states, aux)


def solution(mesh):
    return jax.shard_map(
        body,
        mesh=mesh,
        in_specs=(P("dp", "mp"), P("mp"), P("mp")),
        out_specs=(P("dp", "mp"), P("dp", "mp"), P("dp", "mp")),
        check_vma=False,
    )
```

time: 158 us -> 146 us (0.924); the launches traced: 157 us -> 143 us
  Pallas kernels: 155 us -> 136 us
  local copies, waits for them, and re-layouts: 0.08 us -> 5.7 us
    pallas_call x2 -> x1, Pallas kernels: 155 us -> 136 us  [main(): pl.pallas_call(main_kernel, out_shape=(jax.ShapeDtypeStruct((512, 512), F...]
    unnamed x0 -> x11, local copies, waits for them, and re-layouts: none -> 5.62 us
where the time goes in v3:
time: 146 us; the launch traced here: 143 us
  Pallas kernels  136 us (93%)
  local copies, waits for them, and re-layouts  5.7 us (4%)
    pallas_call x1, Pallas kernels, main(): pl.pallas_call(main_kernel, out_shape=(jax.ShapeDtypeStruct((512, 512), F...  136 us
    unnamed x11, local copies, waits for them, and re-layouts  5.62 us

profile of v3, /device:TPU:1, one launch (start us, length us, event | category | flops | bytes accessed | tf_op | source)
XLA Modules:
  0.0 143.3 jit_solution(4034851719652846821)
XLA Ops:
  0.6 0.0 copy-start.3
  0.7 0.1 pad.2.clone
  0.7 0.6 copy-done.3
  1.3 0.0 copy-start.2
  1.3 0.7 copy-done.2
  2.0 0.7 maximum_maximum_fusion.aux_ref
  2.7 136.3 %window_panel.1 = (f32[512,512]{1,0:T(8,128)}, f32[256,512]{1,0:T(8,128)}, f32[256,512]{1,0:T(8,128)}) custom-call(bf16[1024,512]{1,0:T(8,128)(2,1)} %x_ref.1, f32[8,512]{1,0:T(8,128)} %maximum_maximum_fusion.aux_ref), custom_call_target="tpu_custom_call" | custom-call | tf_op jit(solution)/shard_map/window_panel/pallas_call | solution.py:473
  139.0 0.0 copy-start.1
  139.0 2.3 %copy.9 = f32[512,512]{1,0:T(8,128)} copy(f32[512,512]{1,0:T(8,128)} %get-tuple-element.6) | data formatting | bytes 2097152
  141.3 0.0 copy-done.1
  141.3 0.0 copy-start
  141.3 0.8 copy.10
  142.1 0.4 copy-done
  142.5 0.8 copy.11
  (2 shorter events, 0.0 us)
Async XLA Ops:
  0.6 0.7 copy-start.3
  1.3 0.7 copy-start.2
  139.0 2.3 %copy-start.1 = (f32[256,512]{1,0:T(8,128)S(1)}, f32[256,512]{1,0:T(8,128)}, u32[]{:S(2)}) copy-start(f32[256,512]{1,0:T(8,128)} %get-tuple-element.7) | copy-start | bytes 1572868
  141.3 1.2 copy-start

commit v4 on v3

--- a/solution.py
+++ b/solution.py
@@ -122,6 +122,15 @@
     return jnp.concatenate(done, axis=0)
 
 
+def factor_first(d_ref, li_ref):
+    lane = lax.broadcasted_iota(jnp.int32, (8, 128), 1)
+    sub = lax.broadcasted_iota(jnp.int32, (8, 128), 0)
+    row = lax.broadcasted_iota(jnp.int32, (128, 128), 0)
+    col = lax.broadcasted_iota(jnp.int32, (128, 128), 1)
+    groups = [d_ref[8 * i:8 * i + 8, :] for i in range(16)]
+    li_ref[...] = jnp.where(row >= col, factor_block(groups, lane, sub, lambda p: None), 0.0)
+
+
 def factor_panel(a_ref, d_ref, xl_ref, xr_ref, li_ref, inv_ref, after):
     n, blocks = PANEL, PANEL // 128
     lane = lax.broadcasted_iota(jnp.int32, (8, 128), 1)
@@ -139,13 +148,18 @@
         inv_ref[pl.ds(kb, 128), :] = jnp.where(wide < kb + 128, v, 0.0)
         return v
 
-    d_ref[...] = a_ref[0:128, 0:128]
-    li_ref[...] = jnp.zeros((128, 128), F32)
+    def next_diagonal(k):
+        kb = pl.multiple_of(128 * k, 128)
+        nb = pl.multiple_of(128 * jnp.minimum(k + 1, blocks - 1), 128)
+        v = parts(dot6(li_ref[...], a_ref[pl.ds(kb, 128), pl.ds(nb, 128)]))
+        d_ref[...] = a_ref[pl.ds(nb, 128), pl.ds(nb, 128)] - dot_t(left_of(v, 0), right_of(v, 0))
+
+    next_diagonal(0)
 
     def turn(k, carry):
         kb = pl.multiple_of(128 * k, 128)
         groups = [d_ref[8 * i:8 * i + 8, :] for i in range(16)]
-        prev = jnp.maximum(k - 1, 0)
+        prev = k - 1
         pb = pl.multiple_of(128 * prev, 128)
         v = rows_of(prev)
         xl_ref[...] = left_of(parts(v.T), 1)
@@ -156,7 +170,7 @@
                 return
             top, first = 128 + 448 * ((p - 1) % 2), 256 * ((p - 1) // 2)
             rows, cols = slice(top, top + 448), slice(first, first + 256)
-            below = (top + lax.broadcasted_iota(jnp.int32, (448, 256), 0) >= kb) & (k > 0)
+            below = (top + lax.broadcasted_iota(jnp.int32, (448, 256), 0) >= kb)
             at_col = first + lax.broadcasted_iota(jnp.int32, (448, 256), 1)
             gone = (at_col >= pb) & (at_col < pb + 128)
             old = a_ref[rows, cols]
@@ -165,21 +179,18 @@
             )
             a_ref[rows, cols] = jnp.where(below, new, old)
 
-        li = jnp.where(row >= col, factor_block(groups, lane, sub, hook), 0.0)
-        li_ref[...] = li
-        nb = pl.multiple_of(128 * jnp.minimum(k + 1, blocks - 1), 128)
-        v = parts(dot6(li, a_ref[pl.ds(kb, 128), pl.ds(nb, 128)]))
-        d_ref[...] = a_ref[pl.ds(nb, 128), pl.ds(nb, 128)] - dot_t(left_of(v, 0), right_of(v, 0))
+        li_ref[...] = jnp.where(row >= col, factor_block(groups, lane, sub, hook), 0.0)
+        next_diagonal(k)
         after(k)
         return carry
 
-    lax.fori_loop(0, blocks, turn, 0)
+    lax.fori_loop(1, blocks, turn, 0)
     rows_of(blocks - 1)
 
 
-def main_kernel(x_ref, aux_ref, hess_ref, fac_ref, upd_ref,
+def main_kernel(x_ref, gain_ref, damp_ref, hess_ref, fac_ref, upd_ref,
                 xs, w, auxs, sx, sz, wn, xn, rms, wide, share, share_in, share_sum, share_y, g,
-                slab, other, chip, far, a, d, xl, xr, li, inv, h12, final, extra, h1, hp, hq, u, ss, rs):
+                slab, other, chip, far, a, d, xl, xr, li, inv, h12, final, extra, h1, hp, hq, u, corner, corner_in, corner_sum, corner_far, ss, rs):
     dp, z, h, x = spot()
     c, y = dp % 2, dp // 2
     column = [at(dp, (z + q // 2) % 4, (h + q % 2) % 2, x) for q in range(1, 8)]
@@ -216,8 +227,8 @@
 
     @pl.when(is_source)
     def _():
-        own_damp = [v.astype(F32) for v in parts(aux_ref[1:2, :])]
-        extra_rows = jnp.concatenate([aux_ref[0:1, :]] + own_damp + [jnp.zeros((12, 512), F32)], axis=0)
+        own_damp = [v.astype(F32) for v in parts(damp_ref[...])]
+        extra_rows = jnp.concatenate([gain_ref[...].astype(F32)] + own_damp + [jnp.zeros((12, 512), F32)], axis=0)
         for q in range(8):
             xs[q, 0:16, :] = extra_rows.astype(BF16)
             xs[q, 16:144, :] = x_ref[128 * q:128 * q + 128, :]
@@ -228,23 +239,29 @@
     start(sum_x)
 
     def scatter(q):
-        return copy(xs.at[q], w.at[x, q], q, column[q - 1], 0)
+        return [copy(xs.at[q, pl.ds(p, n)], w.at[x, q, pl.ds(p, n)], 8 * i + q, column[q - 1], i)
+                for i, (p, n) in enumerate([(0, 80), (80, 64)])]
 
     @pl.when(is_source)
     def _():
-        for q in range(1, 8):
-            scatter(q).start()
+        for i in range(2):
+            for q in range(1, 8):
+                scatter(q)[i].start()
 
     own = z * 2 + h
-
-    @pl.when(jnp.logical_not(is_source))
-    def _():
-        copy(xs.at[0], w.at[x, own], 0, column[0], 0).wait_recv()
 
     own_a, own_b = w.at[x, own, pl.ds(0, 80)], w.at[x, own, pl.ds(80, 64)]
     step_2b = [copy(own_b, own_b, 26 + q, column[q - 1]) for q in range(1, 8)]
     step_2a = [copy(own_a, own_a, 24 + j, ring_x[j]) for j in range(3)]
-    start(step_2a + step_2b)
+    def scattered(p, n, i):
+        @pl.when(jnp.logical_not(is_source))
+        def _():
+            copy(xs.at[0, pl.ds(p, n)], w.at[x, own, pl.ds(p, n)], 0, column[0], i).wait_recv()
+
+    scattered(0, 80, 0)
+    start(step_2a)
+    scattered(80, 64, 1)
+    start(step_2b)
     arrive(sum_x)
     sz[own] = (sx[0] + sx[1]) + (sx[2] + sx[3])
     sum_c = [copy(sz.at[own], sz.at[own], 91 + q, column[q - 1]) for q in range(1, 8)]
@@ -267,7 +284,7 @@
     def _(i):
         rows = pl.ds(pl.multiple_of(i * 128, 128), 128)
         scale = jnp.concatenate([rms[rows, :]] * 4, axis=1)
-        xn[rows, :] = (x_ref[rows, :].astype(F32) * scale * aux_ref[0:1, :]).astype(BF16)
+        xn[rows, :] = (x_ref[rows, :].astype(F32) * scale * gain_ref[...].astype(F32)).astype(BF16)
 
     for b in range(4):
         v = w[b, own, 0:16, :].astype(F32)
@@ -302,64 +319,76 @@
         slab[512 * b:512 * b + 512, :] = dot_t(wn[b], xn[...]) * (1.0 / TOKENS)
 
     normalise((0, 1))
+    corner[...] = dot_t(wn[0, :, 0:128], wn[0, :, 0:128]) * (1.0 / TOKENS)
+    corner_core = [copy(corner, corner_in, 99, peer_c)]
+    start(corner_core)
     core_1 = share_of(0)
     normalise((2, 3))
+    core_2 = share_of(1)
+    slab_rows(0)
+    slab_rows(1)
+    spans = [(512 * (1 - c), 0, 512), (1024 + 256 * (1 - c), 512, 256), (1536 + 256 * (1 - c), 768, 256)]
+    slabs = [
+        copy(slab.at[pl.ds(pl.multiple_of(p, 256), n)], other.at[pl.ds(b, n)], 71 + i, peer_c)
+        for i, (p, b, n) in enumerate(spans)
+    ]
+    slab_y = [copy(chip.at[pl.ds(p, 512)], far.at[pl.ds(p, 512)], 73 + i, peer_y)
+              for i, p in ((1, 0), (18, 512))]
+    start(slabs[:1])
     arrive([core_1])
     share_sum[:, panels[0]] = share[keep, panels[0]] + share_in[:, panels[0]]
     to_y = [copy(share_sum.at[:, panels[0]], share_y.at[:, pl.ds(0, 1024)], 55, peer_y)]
     start(to_y)
-    core_2 = share_of(1)
-    slab_rows(0)
-    arrive(to_y)
-    g[z, x, c] = share_sum[:, 0:1024] + share_y[:, 0:1024]
-    first, second = pl.ds(0, 16), pl.ds(16, 16)
-
-    def gather_1(ref, i):
-        one_a, one_b = ref.at[z, x, c, first], ref.at[z, x, c, second]
-        return ([copy(one_a, one_a, i + j, ring_x[j]) for j in range(3)],
-                [copy(one_b, one_b, i + 3 + j, ring_z[j]) for j in range(3)])
-
-    def gather_2(ref, i):
-        row_a, row_b = ref.at[z, :, c, first], ref.at[:, x, c, second]
-        return ([copy(row_a, row_a, i + j, ring_z[j]) for j in range(3)],
-                [copy(row_b, row_b, i + 3 + j, ring_x[j]) for j in range(3)])
-
-    g1, g2 = gather_1(g, 57), gather_2(g, 63)
-    g_core = [copy(g.at[:, :, c, k], g.at[:, :, c, k], i, peer_c) for k, i in ((first, 69), (second, 70))]
-    q1, q2 = gather_1(h12, 75), gather_2(h12, 81)
-    q_core = [copy(h12.at[:, :, c], h12.at[:, :, c], 87, peer_c)]
-    start(g1[0] + g1[1])
+    arrive(corner_core)
+    corner_sum[...] = corner[...] + corner_in[...]
+    corner_y = [copy(corner_sum, corner_far, 100, peer_y)]
+    start(corner_y)
     arrive([core_2])
     share_sum[:, panels[1]] = share[keep, panels[1]] + share_in[:, panels[1]]
     far_12 = pl.ds(pl.multiple_of(1024 + 512 * (1 - y), 512), 512)
     near_12 = pl.ds(pl.multiple_of(1024 + 512 * y, 512), 512)
     to_y2 = [copy(share_sum.at[:, far_12], share_y.at[:, pl.ds(1024, 512)], 56, peer_y)]
     start(to_y2)
-    slab_rows(1)
-    spans = [(512 * (1 - c), 0, 512), (1024 + 256 * (1 - c), 512, 256), (1536 + 256 * (1 - c), 768, 256)]
-    slabs = [
-        copy(slab.at[pl.ds(pl.multiple_of(p, 256), n)], other.at[pl.ds(b, n)], 71 + i, peer_c)
-        for i, (p, b, n) in enumerate(spans)
-    ]
-    start(slabs[:1])
-    slab_y = [copy(chip.at[pl.ds(p, 512)], far.at[pl.ds(p, 512)], 73 + i, peer_y)
-              for i, p in ((1, 0), (18, 512))]
+    arrive(slabs[:1])
+    chip[0:512, :] = slab[pl.ds(pl.multiple_of(512 * c, 512), 512), :] + other[0:512, :]
+    start(slab_y[:1])
+    arrive(to_y)
+    g[z, x, c] = share_sum[:, 0:1024] + share_y[:, 0:1024]
+    first, second = pl.ds(0, 16), pl.ds(16, 16)
+
+    def gather_1(ref, i):
+        one_a, one_b = ref.at[z, x, c, first], ref.at[z, x, c, second]
+        return ([copy(one_a, one_a, i + j, ring_x[j]) for j in range(3)],
+                [copy(one_b, one_b, i + 3 + j, ring_z[j]) for j in range(3)])
+
+    def gather_2(ref, i):
+        row_a, row_b = ref.at[z, :, c, first], ref.at[:, x, c, second]
+        return ([copy(row_a, row_a, i + j, ring_z[j]) for j in range(3)],
+                [copy(row_b, row_b, i + 3 + j, ring_x[j]) for j in range(3)])
+
+    g1, g2 = gather_1(g, 57), gather_2(g, 63)
+    g_core = [copy(g.at[:, :, c, k], g.at[:, :, c, k], i, peer_c) for k, i in ((first, 69), (second, 70))]
+    q1, q2 = gather_1(h12, 75), gather_2(h12, 81)
+    q_core = [copy(h12.at[:, :, c], h12.at[:, :, c], 87, peer_c)]
+    start(g1[0] + g1[1])
+    slab_rows(2)
+    slab_rows(3)
+    start(slabs[1:])
+    row = lax.broadcasted_iota(jnp.int32, (128, 128), 0)
+    col = lax.broadcasted_iota(jnp.int32, (128, 128), 1)
     arrive(g1[0])
     start(g2[0])
     arrive(g1[1])
     start(g2[1])
-    slab_rows(2)
-    slab_rows(3)
-    start(slabs[1:])
     arrive(to_y2)
     h12[z, x, c] = share_sum[:, near_12] + share_y[:, 1024:1536]
-    arrive(slabs[:1])
-    chip[0:512, :] = slab[pl.ds(pl.multiple_of(512 * c, 512), 512), :] + other[0:512, :]
-    start(slab_y[:1])
     arrive(slabs[1:])
     chip[512:768, :] = slab[pl.ds(pl.multiple_of(1024 + 256 * c, 256), 256), :] + other[512:768, :]
     chip[768:1024, :] = slab[pl.ds(pl.multiple_of(1536 + 256 * c, 256), 256), :] + other[768:1024, :]
     start(slab_y[1:])
+    arrive(corner_y)
+    d[...] = corner_sum[...] + corner_far[...] + jnp.where(row == col, auxs[0, 1:2, 0:128], 0.0)
+    factor_first(d, li)
     arrive(g2[0])
     start(g_core[:1])
     arrive(g2[1])
@@ -371,8 +400,6 @@
             for k in range(2):
                 lo = 64 * (4 * i + j) + 32 * k
                 a[lo:lo + 32, :] = g[i, j, k]
-    row = lax.broadcasted_iota(jnp.int32, (128, 128), 0)
-    col = lax.broadcasted_iota(jnp.int32, (128, 128), 1)
     for k in range(8):
         at_k = slice(128 * k, 128 * k + 128)
         damp = auxs[k // 4, 1:2, 128 * (k % 4):128 * (k % 4) + 128]
@@ -397,7 +424,7 @@
             for m in q_core:
                 m.start()
 
-        @pl.when(k == 5)
+        @pl.when(k == 6)
         def _():
             arrive(slab_y)
             final[...] = chip[...] + far[...]
@@ -408,7 +435,7 @@
     arrive(q_core + to_e)
 
     first_col = (z * 8 + h * 4 + x) * 512
-    damp_own = aux_ref[1:2, :]
+    damp_own = damp_ref[...]
 
     def damped(value, first_row):
         rows = first_row + lax.broadcasted_iota(jnp.int32, value.shape, 0)
@@ -460,10 +487,11 @@
     @pl.when(is_source)
     def _():
         for q in range(1, 8):
-            scatter(q).wait_send()
-
-
-def main(hidden, aux):
+            for k in scatter(q):
+                k.wait_send()
+
+
+def main(hidden, gain, damping):
     def f32(*shape):
         return pltpu.VMEM(shape, F32)
 
@@ -477,7 +505,7 @@
             jax.ShapeDtypeStruct((256, 512), F32),
             jax.ShapeDtypeStruct((256, 512), F32),
         ),
-        in_specs=[VM, VM],
+        in_specs=[VM, VM, VM],
         out_specs=(VM, VM, VM),
         scratch_shapes=[
             b16(8, 144, 512), b16(4, 8, 144, 512), f32(4, 8, 512), f32(4, 8, 128), f32(8, 8, 128),
@@ -487,19 +515,17 @@
             f32(PANEL, PANEL), f32(128, 128), b16(PANEL, 768), b16(768, PANEL), f32(128, 128),
             f32(PANEL, PANEL), f32(4, 4, 2, 32, 512), f32(1024, 512), f32(768, 512),
             f32(1024, 512), b16(1024, 768), b16(1024, 768), f32(1024, 768),
-            pltpu.SemaphoreType.DMA((100,)),
-            pltpu.SemaphoreType.DMA((100,)),
+            f32(128, 128), f32(128, 128), f32(128, 128), f32(128, 128),
+            pltpu.SemaphoreType.DMA((101,)),
+            pltpu.SemaphoreType.DMA((101,)),
         ],
         compiler_params=params(collective_id=0, has_side_effects=True),
         name="window_panel",
-    )(hidden, aux)
+    )(hidden, gain, damping)
 
 
 def body(hidden_states, norm_gain, damping):
-    aux = jnp.concatenate(
-        [norm_gain.astype(F32)[None], damping[None], jnp.zeros((6, norm_gain.shape[0]), F32)], axis=0
-    )
-    return main(hidden_states, aux)
+    return main(hidden_states, norm_gain[None], damping[None])
 
 
 def solution(mesh):

time: 146 us -> 138 us (0.945)
  Pallas kernels: 136 us -> 130 us
    pallas_call x1, Pallas kernels: 136 us -> 130 us  [main(): pl.pallas_call(main_kernel, out_shape=(jax.ShapeDtypeStruct((512, 512), F...]
    unnamed x11 -> x9, local copies, waits for them, and re-layouts: 5.62 us -> 5.02 us
where the time goes in v4:
time: 138 us; the launch traced here: 136 us
  Pallas kernels  130 us (94%)
  local copies, waits for them, and re-layouts  5.6 us (4%)
    pallas_call x1, Pallas kernels, main(): pl.pallas_call(main_kernel, out_shape=(jax.ShapeDtypeStruct((512, 512), F...  130 us
    unnamed x9, local copies, waits for them, and re-layouts  5.02 us

profile of v4, /device:TPU:1, one launch (start us, length us, event | category | flops | bytes accessed | tf_op | source)
XLA Modules:
  0.0 136.3 jit_solution(680601305588839372)
XLA Ops:
  0.6 0.0 copy-start.2
  0.6 0.7 copy-done.2
  1.3 0.6 broadcast_in_dim.6.gain_ref
  1.9 130.0 %window_panel.1 = (f32[512,512]{1,0:T(8,128)}, f32[256,512]{1,0:T(8,128)}, f32[256,512]{1,0:T(8,128)}) custom-call(bf16[1024,512]{1,0:T(8,128)(2,1)} %x_ref.1, bf16[1,512]{1,0:T(2,128)(2,1)} %broadcast_in_dim.6.gain_ref, f32[1,512]{1,0:T(1,128)} %bitcast.1), custom_call_target="tpu_custom_call" | custom-call | tf_op jit(solution)/shard_map/window_panel/pallas_call | solution.py:501
  131.9 0.0 copy-start.1
  131.9 2.3 %copy.9 = f32[512,512]{1,0:T(8,128)} copy(f32[512,512]{1,0:T(8,128)} %get-tuple-element.6) | data formatting | bytes 2097152
  134.2 0.0 copy-done.1
  134.2 0.0 copy-start
  134.2 0.8 copy.10
  135.0 0.4 copy-done
  135.5 0.8 copy.11
Async XLA Ops:
  0.6 0.7 copy-start.2
  131.9 2.3 %copy-start.1 = (f32[256,512]{1,0:T(8,128)S(1)}, f32[256,512]{1,0:T(8,128)}, u32[]{:S(2)}) copy-start(f32[256,512]{1,0:T(8,128)} %get-tuple-element.7) | copy-start | bytes 1572868
  134.2 1.2 copy-start

commit v5 on v4

--- a/solution.py
+++ b/solution.py
@@ -232,15 +232,15 @@
         for q in range(8):
             xs[q, 0:16, :] = extra_rows.astype(BF16)
             xs[q, 16:144, :] = x_ref[128 * q:128 * q + 128, :]
-        w[x, 0] = xs[0]
+        w[x, 0, 0] = xs[0]
 
     greet_wait(12)
     sum_x = [copy(sx.at[x], sx.at[x], 47 + j, ring_x[j]) for j in range(3)]
     start(sum_x)
 
     def scatter(q):
-        return [copy(xs.at[q, pl.ds(p, n)], w.at[x, q, pl.ds(p, n)], 8 * i + q, column[q - 1], i)
-                for i, (p, n) in enumerate([(0, 80), (80, 64)])]
+        return [copy(xs.at[q, pl.ds(p, n)], w.at[x, q // 2, q % 2, pl.ds(p, n)], 8 * i + q, column[q - 1], i)
+                for i, (p, n) in enumerate([(0, 96), (96, 48)])]
 
     @pl.when(is_source)
     def _():
@@ -250,29 +250,40 @@
 
     own = z * 2 + h
 
-    own_a, own_b = w.at[x, own, pl.ds(0, 80)], w.at[x, own, pl.ds(80, 64)]
+    arrive(sum_x)
+    sz[own] = (sx[0] + sx[1]) + (sx[2] + sx[3])
+    sum_c = [copy(sz.at[own], sz.at[own], 91 + q, column[q - 1]) for q in range(1, 8)]
+    start(sum_c)
+
+    own_a, own_b = w.at[x, z, h, pl.ds(0, 96)], w.at[x, z, h, pl.ds(96, 48)]
     step_2b = [copy(own_b, own_b, 26 + q, column[q - 1]) for q in range(1, 8)]
     step_2a = [copy(own_a, own_a, 24 + j, ring_x[j]) for j in range(3)]
     def scattered(p, n, i):
         @pl.when(jnp.logical_not(is_source))
         def _():
-            copy(xs.at[0, pl.ds(p, n)], w.at[x, own, pl.ds(p, n)], 0, column[0], i).wait_recv()
-
-    scattered(0, 80, 0)
+            copy(xs.at[0, pl.ds(p, n)], w.at[x, z, h, pl.ds(p, n)], 0, column[0], i).wait_recv()
+
+    scattered(0, 96, 0)
     start(step_2a)
-    scattered(80, 64, 1)
+    scattered(96, 48, 1)
     start(step_2b)
-    arrive(sum_x)
-    sz[own] = (sx[0] + sx[1]) + (sx[2] + sx[3])
-    sum_c = [copy(sz.at[own], sz.at[own], 91 + q, column[q - 1]) for q in range(1, 8)]
-    start(sum_c)
-    all_a, all_b = w.at[:, own, pl.ds(16, 64)], w.at[x, :, pl.ds(80, 64)]
-    step_3a = [copy(all_a, all_a, 36 + q, column[q - 1]) for q in range(1, 8)]
+    all_b = w.at[x, :, :, pl.ds(96, 48)]
+    over_z, over_h = w.at[:, z, h, pl.ds(16, 48)], w.at[:, z, h, pl.ds(64, 32)]
+    then_h, then_z = w.at[:, :, h, pl.ds(16, 48)], w.at[:, z, :, pl.ds(64, 32)]
+    peer_h = at(dp, z, 1 - h, x)
+    step_3z = [copy(over_z, over_z, 36 + j, ring_z[j]) for j in range(3)]
+    step_3h = [copy(over_h, over_h, 39, peer_h)]
+    step_4h = [copy(then_h, then_h, 40, peer_h)]
+    step_4z = [copy(then_z, then_z, 41 + j, ring_z[j]) for j in range(3)]
     step_3b = [copy(all_b, all_b, 44 + j, ring_x[j]) for j in range(3)]
     arrive(step_2a)
-    start(step_3a)
+    start(step_3z + step_3h)
     arrive(step_2b)
     start(step_3b)
+    arrive(step_3h)
+    start(step_4z)
+    arrive(step_3z)
+    start(step_4h)
     arrive(sum_c)
 
     total = ((sz[0] + sz[1]) + (sz[2] + sz[3])) + ((sz[4] + sz[5]) + (sz[6] + sz[7]))
@@ -287,10 +298,10 @@
         xn[rows, :] = (x_ref[rows, :].astype(F32) * scale * gain_ref[...].astype(F32)).astype(BF16)
 
     for b in range(4):
-        v = w[b, own, 0:16, :].astype(F32)
+        v = w[b, z, h, 0:16, :].astype(F32)
         auxs[b, 0:1, :] = v[0:1, :]
         auxs[b, 1:2, :] = (v[1:2, :] + v[2:3, :]) + v[3:4, :]
-    arrive(step_3a)
+    arrive(step_4z + step_4h)
     arrive(step_3b)
 
     def normalise(blocks):
@@ -299,7 +310,7 @@
             rows = pl.ds(pl.multiple_of(i * 128, 128), 128)
             scale = jnp.concatenate([rms[rows, :]] * 4, axis=1)
             for b in blocks:
-                wn[b, rows, :] = (w[b, i, 16:144, :].astype(F32) * scale * auxs[b, 0:1, :]).astype(BF16)
+                wn[b, rows, :] = (w[b, i // 2, i % 2, 16:144, :].astype(F32) * scale * auxs[b, 0:1, :]).astype(BF16)
 
     s = z * 4 + x
     half = pl.ds(pl.multiple_of((s % 2) * 64, 64), 64)
@@ -508,7 +519,7 @@
         in_specs=[VM, VM, VM],
         out_specs=(VM, VM, VM),
         scratch_shapes=[
-            b16(8, 144, 512), b16(4, 8, 144, 512), f32(4, 8, 512), f32(4, 8, 128), f32(8, 8, 128),
+            b16(8, 144, 512), b16(4, 4, 2, 144, 512), f32(4, 8, 512), f32(4, 8, 128), f32(8, 8, 128),
             b16(4, 1024, 512), b16(1024, 512), f32(1024, 128), f32(128, 1024), f32(64, 2048),
             f32(32, 2048), f32(32, 2048), f32(32, 1536), f32(4, 4, 2, 32, 1024),
             f32(2048, 512), f32(1024, 512), f32(1024, 512), f32(1024, 512),

time: 138 us -> 135 us (0.978); the launches traced: 136 us -> 135 us
  no operation moved by 1% of the time
where the time goes in v5:
time: 135 us
  Pallas kernels  129 us (96%)
  local copies, waits for them, and re-layouts  5.6 us (4%)
    pallas_call x1, Pallas kernels, main(): pl.pallas_call(main_kernel, out_shape=(jax.ShapeDtypeStruct((512, 512), F...  129 us
    unnamed x9, local copies, waits for them, and re-layouts  5.02 us

profile of v5, /device:TPU:1, one launch (start us, length us, event | category | flops | bytes accessed | tf_op | source)
XLA Modules:
  0.0 134.9 jit_solution(17839273486658414789)
XLA Ops:
  0.6 0.0 copy-start.2
  0.6 0.7 copy-done.2
  1.3 0.6 broadcast_in_dim.6.gain_ref
  1.9 128.7 %window_panel.1 = (f32[512,512]{1,0:T(8,128)}, f32[256,512]{1,0:T(8,128)}, f32[256,512]{1,0:T(8,128)}) custom-call(bf16[1024,512]{1,0:T(8,128)(2,1)} %x_ref.1, bf16[1,512]{1,0:T(2,128)(2,1)} %broadcast_in_dim.6.gain_ref, f32[1,512]{1,0:T(1,128)} %bitcast.1), custom_call_target="tpu_custom_call" | custom-call | tf_op jit(solution)/shard_map/window_panel/pallas_call | solution.py:512
  130.6 0.0 copy-start.1
  130.6 2.3 %copy.9 = f32[512,512]{1,0:T(8,128)} copy(f32[512,512]{1,0:T(8,128)} %get-tuple-element.6) | data formatting | bytes 2097152
  132.9 0.0 copy-done.1
  132.9 0.0 copy-start
  132.9 0.8 copy.10
  133.7 0.4 copy-done
  134.1 0.8 copy.11
Async XLA Ops:
  0.6 0.7 copy-start.2
  130.6 2.3 %copy-start.1 = (f32[256,512]{1,0:T(8,128)S(1)}, f32[256,512]{1,0:T(8,128)}, u32[]{:S(2)}) copy-start(f32[256,512]{1,0:T(8,128)} %get-tuple-element.7) | copy-start | bytes 1572868
  132.9 1.2 copy-start

commit v6 on v5

--- a/solution.py
+++ b/solution.py
@@ -278,10 +278,10 @@
     step_3b = [copy(all_b, all_b, 44 + j, ring_x[j]) for j in range(3)]
     arrive(step_2a)
     start(step_3z + step_3h)
+    arrive(step_3h)
+    start(step_4z)
     arrive(step_2b)
     start(step_3b)
-    arrive(step_3h)
-    start(step_4z)
     arrive(step_3z)
     start(step_4h)
     arrive(sum_c)

time: 135 us -> 135 us (level)
  no operation moved by 1% of the time
where the time goes in v6:
time: 135 us
  Pallas kernels  129 us (96%)
  local copies, waits for them, and re-layouts  5.6 us (4%)
    pallas_call x1, Pallas kernels, main(): pl.pallas_call(main_kernel, out_shape=(jax.ShapeDtypeStruct((512, 512), F...  129 us
    unnamed x9, local copies, waits for them, and re-layouts  5.02 us

profile of v6, /device:TPU:1, one launch (start us, length us, event | category | flops | bytes accessed | tf_op | source)
XLA Modules:
  0.0 134.9 jit_solution(10127213101203741545)
XLA Ops:
  0.6 0.0 copy-start.2
  0.6 0.7 copy-done.2
  1.3 0.6 broadcast_in_dim.6.gain_ref
  1.9 128.7 %window_panel.1 = (f32[512,512]{1,0:T(8,128)}, f32[256,512]{1,0:T(8,128)}, f32[256,512]{1,0:T(8,128)}) custom-call(bf16[1024,512]{1,0:T(8,128)(2,1)} %x_ref.1, bf16[1,512]{1,0:T(2,128)(2,1)} %broadcast_in_dim.6.gain_ref, f32[1,512]{1,0:T(1,128)} %bitcast.1), custom_call_target="tpu_custom_call" | custom-call | tf_op jit(solution)/shard_map/window_panel/pallas_call | solution.py:512
  130.6 0.0 copy-start.1
  130.6 2.3 %copy.9 = f32[512,512]{1,0:T(8,128)} copy(f32[512,512]{1,0:T(8,128)} %get-tuple-element.6) | data formatting | bytes 2097152
  132.9 0.0 copy-done.1
  132.9 0.0 copy-start
  132.9 0.8 copy.10
  133.7 0.4 copy-done
  134.1 0.8 copy.11
Async XLA Ops:
  0.6 0.7 copy-start.2
  130.6 2.3 %copy-start.1 = (f32[256,512]{1,0:T(8,128)S(1)}, f32[256,512]{1,0:T(8,128)}, u32[]{:S(2)}) copy-start(f32[256,512]{1,0:T(8,128)} %get-tuple-element.7) | copy-start | bytes 1572868
  132.9 1.2 copy-start
